TPU v7x, 32 devices: a whole 2x2x4 slice. The times are simulated.
32 devices in a mesh: seq: 16 (over z, x, core), tp: 2 (over y).
Axes of the slice: x: 2, y: 2, z: 4, core: 2. Of those that a mesh axis runs over, the one named last changes fastest.
Arguments:
- acts: bfloat16 [8192, 4608], P('seq', 'tp'), may hold values from -6 to 6
- attn: bfloat16 [8192, 4096], P('seq', 'tp'), may hold values from -6 to 6
- teacher: bfloat16 [8192, 3584], P('seq', 'tp'), may hold values from -6 to 6
- out_weight: bfloat16 [4096, 4608], P('tp'), may hold values from -0.09375 to 0.09375
- proj_weight: bfloat16 [3584, 4608], P('tp'), may hold values from -0.09375 to 0.09375
Outputs:
- attn_grad: bfloat16 [8192, 4096], P('seq', 'tp')
- out_grad: bfloat16 [4096, 4608], P('tp', 'seq')
- proj_grad: bfloat16 [3584, 4608], P('tp', 'seq')
All inputs are finite; a program needn't handle non-finite values.
Results may differ from a plain program's by a relative error of at most 0.015.
Values may be sent and summed in bfloat16 or wider, within the bound.
A program may use at most 192 MiB of HBM per device.

v0:
```python
import jax
import jax.numpy as jnp
from jax import lax
from jax.sharding import PartitionSpec as P


def local(acts, attn, teacher, out_weight, proj_weight):
    joined = jnp.dot(attn, out_weight, preferred_element_type=jnp.float32) - jnp.dot(
        teacher, proj_weight, preferred_element_type=jnp.float32
    )
    totals = lax.psum(joined.astype(jnp.bfloat16), "tp").astype(jnp.float32)
    whole_acts = lax.all_gather(acts, "tp", axis=1, tiled=True)
    resid_grad = (whole_acts.astype(jnp.float32) + totals).astype(jnp.bfloat16)
    attn_grad = lax.dot_general(
        resid_grad, out_weight, (((1,), (1,)), ((), ())), preferred_element_type=jnp.float32
    ).astype(jnp.bfloat16)
    out_terms = lax.dot_general(
        attn, resid_grad, (((0,), (0,)), ((), ())), preferred_element_type=jnp.float32
    )
    proj_terms = -lax.dot_general(
        teacher, resid_grad, (((0,), (0,)), ((), ())), preferred_element_type=jnp.float32
    )
    out_grad, proj_grad = (
        lax.psum_scatter(
            out_terms.astype(jnp.bfloat16), "seq", scatter_dimension=1, tiled=True
        ).astype(jnp.float32),
        lax.psum_scatter(
            proj_terms.astype(jnp.bfloat16), "seq", scatter_dimension=1, tiled=True
        ).astype(jnp.float32),
    )
    return (attn_grad, out_grad.astype(jnp.bfloat16), proj_grad.astype(jnp.bfloat16))


def solution(mesh):
    placed = (P("seq", "tp"), P("seq", "tp"), P("seq", "tp"), P("tp", None), P("tp", None))
    return jax.shard_map(
        local,
        mesh=mesh,
        in_specs=placed,
        out_specs=(P("seq", "tp"), P("tp", "seq"), P("tp", "seq")),
        check_vma=False,
    )
```

profile of v0, /device:TPU:0, one launch (start us, length us, event | category | flops | bytes accessed | tf_op | source)
XLA Modules:
  0.0 618.2 jit_solution(1499089932930985267)
XLA Ops:
  7.2 0.0 copy-start
  7.2 0.0 all-reduce.2.cloned.1.call-start
  7.2 12.3 %fusion.2 = f32[512,4608]{1,0:T(8,128)S(1)} fusion(bf16[512,1792]{1,0:T(8,128)(2,1)} %param.7, bf16[1792,4608]{1,0:T(8,128)(2,1)} %param.9), kind=kOutput, calls=%fused_computation.7 | convolution fusion | flops 8455716864 | bytes 27787264 | tf_op jit(solution)/shard_map/dot_general | solution.py:8
  19.6 0.0 copy-done
  19.6 15.3 %subtract_convert_fusion = bf16[512,4608]{1,0:T(8,128)(2,1)} fusion(f32[512,4608]{1,0:T(8,128)S(1)} %fusion.2, bf16[512,2048]{1,0:T(8,128)(2,1)S(1)} %copy-done, bf16[2048,4608]{1,0:T(8,128)(2,1)} %param.8), kind=kOutput, calls=%fused_computation.5 | convolution fusion | flops 9668395008 | bytes 35127296 | tf_op jit(solution)/shard_map/dot_general | solution.py:8
  34.9 0.0 all-reduce.2.cloned.1.call-update
  34.9 0.0 all-gather.2.cloned.1.call-start
  35.0 0.7 all-gather.2.cloned.1.call-update
  35.7 0.0 reduce-scatter.5.cloned.1.call-start
  35.7 121.3 %all-reduce.2.cloned.1.call-done = bf16[512,4608]{1,0:T(8,128)(2,1)} async-done(((bf16[512,4608]{1,0:T(8,128)(2,1)}), bf16[512,4608]{1,0:T(8,128)(2,1)}) %all-reduce.2.cloned.1.call-update) | async-done | bytes 4718608 | tf_op jit(solution)/shard_map/psum | solution.py:11
  157.0 64.3 %all-gather.2.cloned.1.call-done = bf16[512,4608]{1,0:T(8,128)(2,1)} async-done(((bf16[512,2304]{1,0:T(8,128)(2,1)}), bf16[512,4608]{1,0:T(8,128)(2,1)}) %all-gather.2.cloned.1.call-update) | async-done | bytes 4718608 | tf_op jit(solution)/shard_map/all_gather | solution.py:12
  221.3 15.1 %fusion.1 = bf16[1792,4608]{0,1:T(8,128)(2,1)} fusion(bf16[512,1792]{1,0:T(8,128)(2,1)} %param.7, bf16[512,4608]{1,0:T(8,128)(2,1)} %all-reduce.2.cloned.1.call-done, bf16[512,4608]{1,0:T(8,128)(2,1)} %all-gather.2.cloned.1.call-done), kind=kOutput, calls=%fused_computation.3 | convolution fusion | flops 8481669120 | bytes 27787264 | tf_op jit(solution)/shard_map/dot_general | solution.py:20
  236.4 0.0 reduce-scatter.5.cloned.1.call-update
  236.5 0.2 reduce-scatter.3.cloned.1.call-start
  236.7 17.0 %fusion = bf16[2048,4608]{0,1:T(8,128)(2,1)} fusion(bf16[512,2048]{1,0:T(8,128)(2,1)S(1)} %copy-done, bf16[512,4608]{1,0:T(8,128)(2,1)} %all-reduce.2.cloned.1.call-done, bf16[512,4608]{1,0:T(8,128)(2,1)} %all-gather.2.cloned.1.call-done), kind=kOutput, calls=%fused_computation.2 | convolution fusion | flops 9682550784 | bytes 30408704 | tf_op jit(solution)/shard_map/dot_general | solution.py:17
  253.7 0.0 reduce-scatter.3.cloned.1.call-update
  253.7 0.0 copy-start.1
  253.7 20.9 %convolution_convert_fusion.1 = bf16[512,2048]{1,0:T(8,128)(2,1)} fusion(bf16[2048,4608]{1,0:T(8,128)(2,1)} %param.8, bf16[512,4608]{1,0:T(8,128)(2,1)} %all-reduce.2.cloned.1.call-done, bf16[512,4608]{1,0:T(8,128)(2,1)} %all-gather.2.cloned.1.call-done), kind=kOutput, calls=%fused_computation.6 | convolution fusion | flops 9674162176 | bytes 30408704 | tf_op jit(solution)/shard_map/dot_general | solution.py:14
  274.6 138.5 %reduce-scatter.5.cloned.1.call-done = bf16[1792,288]{0,1:T(8,128)(2,1)} async-done(((bf16[1792,4608]{0,1:T(8,128)(2,1)}), bf16[1792,288]{0,1:T(8,128)(2,1)}) %reduce-scatter.5.cloned.1.call-update) | async-done | bytes 1032208 | tf_op jit(solution)/shard_map/reduce_scatter | solution.py:27
  413.2 198.5 %reduce-scatter.3.cloned.1.call-done = bf16[2048,288]{0,1:T(8,128)(2,1)} async-done(((bf16[2048,4608]{0,1:T(8,128)(2,1)}), bf16[2048,288]{0,1:T(8,128)(2,1)}) %reduce-scatter.3.cloned.1.call-update) | async-done | bytes 1179664 | tf_op jit(solution)/shard_map/reduce_scatter | solution.py:24
  611.7 0.0 copy-done.1
Async XLA Ops:
  7.2 12.4 %copy-start = (bf16[512,2048]{1,0:T(8,128)(2,1)S(1)}, bf16[512,2048]{1,0:T(8,128)(2,1)}, u32[]{:S(2)}) copy-start(bf16[512,2048]{1,0:T(8,128)(2,1)} %param.6) | copy-start | bytes 6291460
  7.2 149.8 %all-reduce.2.cloned.1.call-start = ((), (), s32[]{:S(2)}) async-start(), calls=%async_computation.3 | async-start | bytes 9437184 | tf_op jit(solution)/shard_map/psum | solution.py:11
  34.9 186.4 %all-gather.2.cloned.1.call-start = ((), (), s32[]{:S(2)}) async-start(), calls=%async_computation.2 | async-start | bytes 7077888 | tf_op jit(solution)/shard_map/all_gather | solution.py:12
  35.7 377.5 %reduce-scatter.5.cloned.1.call-start = ((), (), s32[]{:S(2)}) async-start(), calls=%async_computation.5 | async-start | bytes 17547264 | tf_op jit(solution)/shard_map/reduce_scatter | solution.py:27
  236.5 375.2 %reduce-scatter.3.cloned.1.call-start = ((), (), s32[]{:S(2)}) async-start(), calls=%async_computation.4 | async-start | bytes 20054016 | tf_op jit(solution)/shard_map/reduce_scatter | solution.py:24
  253.7 358.0 %copy-start.1 = (bf16[512,2048]{1,0:T(8,128)(2,1)S(1)}, bf16[512,2048]{1,0:T(8,128)(2,1)}, u32[]{:S(2)}) copy-start(bf16[512,2048]{1,0:T(8,128)(2,1)} %param.6) | copy-start | bytes 6291460
Sparse Core Ops, SparseCore 0:
  35.0 121.9 all-reduce.1
  158.6 62.6 all-gather.1
  236.6 176.5 reduce-scatter.4
  417.7 193.9 reduce-scatter.2
where the time goes:
time: 618 us
  waiting for transfers between devices  523 us (85%)
  matrix products  80.7 us (13%)
  between operations  13.8 us (2%)
    reduce_scatter x1, waiting for transfers between devices, local(): lax.psum_scatter(out_terms.astype(jnp.bfloat16), 'seq', scatter_dimension...  198 us
    reduce_scatter x1, waiting for transfers between devices, local(): lax.psum_scatter(proj_terms.astype(jnp.bfloat16), 'seq', scatter_dimensio...  139 us
    psum x1, waiting for transfers between devices, local(): totals = lax.psum(joined.astype(jnp.bfloat16), 'tp').astype(jnp.float32)  121 us
    all_gather x1, waiting for transfers between devices, local(): whole_acts = lax.all_gather(acts, 'tp', axis=1, tiled=True)  64.3 us
    dot_general x1, matrix products, local(): lax.dot_general(resid_grad, out_weight, (((1,), (1,)), ((), ())), preferr...  20.9 us
    dot_general x1, matrix products, local(): lax.dot_general(attn, resid_grad, (((0,), (0,)), ((), ())), preferred_ele...  17 us
    dot_general x1, matrix products, local(): jnp.dot(attn, out_weight, preferred_element_type=jnp.float32)  15.3 us
    dot_general x1, matrix products, local(): lax.dot_general(teacher, resid_grad, (((0,), (0,)), ((), ())), preferred_...  15.1 us
  transfers between devices with their start and end apart: 4, of which 4 were waited for; matrix products, arithmetic and copies ran while one was open for 6% of the time, Pallas kernels for 0%

commit v1 on v0

v1 whole, which is shorter than its diff:
```python
import functools

import jax
import jax.numpy as jnp
from jax import lax
from jax.sharding import PartitionSpec as P

F32 = jnp.float32
BF16 = jnp.bfloat16


def generic(acts, attn, teacher, out_weight, proj_weight):
    joined = jnp.dot(attn, out_weight, preferred_element_type=F32) - jnp.dot(
        teacher, proj_weight, preferred_element_type=F32
    )
    totals = lax.psum(joined.astype(BF16), "tp").astype(F32)
    whole_acts = lax.all_gather(acts, "tp", axis=1, tiled=True)
    resid_grad = (whole_acts.astype(F32) + totals).astype(BF16)
    attn_grad = lax.dot_general(
        resid_grad, out_weight, (((1,), (1,)), ((), ())), preferred_element_type=F32
    ).astype(BF16)
    out_terms = lax.dot_general(
        attn, resid_grad, (((0,), (0,)), ((), ())), preferred_element_type=F32
    )
    proj_terms = -lax.dot_general(
        teacher, resid_grad, (((0,), (0,)), ((), ())), preferred_element_type=F32
    )
    return (
        attn_grad,
        lax.psum_scatter(out_terms.astype(BF16), "seq", scatter_dimension=1, tiled=True),
        lax.psum_scatter(proj_terms.astype(BF16), "seq", scatter_dimension=1, tiled=True),
    )


def add(a, b):
    return (a.astype(F32) + b.astype(F32)).astype(BF16)


def local(acts, attn, teacher, out_weight, proj_weight):
    s = lax.axis_index("seq")
    tp = lax.axis_index("tp")
    core, x, z = s % 2, (s // 2) % 2, s // 4
    ds = out_weight.shape[1]
    width = ds // 4
    strip = width // 4
    half = acts.shape[1]
    features = attn.shape[1]
    both = jnp.concatenate([attn, -teacher], axis=1)
    core_pairs = [(i, i ^ 1) for i in range(16)]
    x_pairs = [(i, i ^ 2) for i in range(16)]
    hops = {
        0: [[(3, 2)], [(2, 1)], [(1, 0)]],
        1: [[(3, 2), (0, 1)], [(2, 1)]],
        2: [[(0, 1), (3, 2)], [(1, 2)]],
        3: [[(0, 1)], [(1, 2)], [(2, 3)]],
    }
    order = [0, 3, 1, 2]
    resid = {}
    for k in order:
        cols = slice(k * width, (k + 1) * width)
        part = jnp.dot(attn, out_weight[:, cols], preferred_element_type=F32) - jnp.dot(
            teacher, proj_weight[:, cols], preferred_element_type=F32
        )
        own, at = divmod(k * width, half)
        mine = jnp.where(tp == own, acts[:, at : at + width].astype(F32), 0.0)
        part = (part + mine).astype(BF16)
        other = lax.ppermute(part, "tp", [(0, 1), (1, 0)])
        resid[k] = add(part, other)
    total = None
    for k in order:
        terms = lax.dot_general(
            resid[k], both, (((0,), (0,)), ((), ())), preferred_element_type=F32
        ).astype(BF16)
        terms = terms.reshape(2, 2, strip, -1)
        keep = lax.dynamic_index_in_dim(terms, core, 1, keepdims=False)
        send = lax.dynamic_index_in_dim(terms, 1 - core, 1, keepdims=False)
        chip = add(keep, lax.ppermute(send, "seq", core_pairs))
        keep = lax.dynamic_index_in_dim(chip, x, 0, keepdims=False)
        send = lax.dynamic_index_in_dim(chip, 1 - x, 0, keepdims=False)
        line = add(keep, lax.ppermute(send, "seq", x_pairs))
        for hop in hops[k]:
            pairs = [(a * 4 + i, b * 4 + i) for a, b in hop for i in range(4)]
            line = add(line, lax.ppermute(line, "seq", pairs))
        total = line if total is None else jnp.where(z == k, line, total)
    whole = jnp.concatenate([resid[k] for k in range(4)], axis=1)
    attn_grad = lax.dot_general(
        whole, out_weight, (((1,), (1,)), ((), ())), preferred_element_type=F32
    ).astype(BF16)
    total = total.T
    return attn_grad, total[:features], total[features:]


def solution(mesh):
    placed = (P("seq", "tp"), P("seq", "tp"), P("seq", "tp"), P("tp", None), P("tp", None))
    tuned = mesh.shape["seq"] == 16 and mesh.shape["tp"] == 2
    return jax.shard_map(
        local if tuned else generic,
        mesh=mesh,
        in_specs=placed,
        out_specs=(P("seq", "tp"), P("tp", "seq"), P("tp", "seq")),
        check_vma=False,
    )
```

time: 618 us -> 523 us (0.85); the launches traced: 618 us -> 514 us
  waiting for transfers between devices: 523 us -> 308 us
  other arithmetic: 0 us -> 50.7 us
  starting transfers between devices: 0.34 us -> 29.8 us
  local copies, waits for them, and re-layouts: 0.02 us -> 23.7 us
  matrix products: 80.7 us -> 100 us
  between operations: 13.8 us -> 1.19 us
    reduce_scatter x2 -> x0, waiting for transfers between devices: 337 us -> none  [the longest x1 198 us: local(): lax.psum_scatter(out_terms.astype(jnp.bfloat16), 'seq', scatter_dimension...]
    ppermute x0 -> x22, waiting for transfers between devices: none -> 308 us  [the longest x4 158 us: local(): line = add(keep, lax.ppermute(send, 'seq', x_pairs))]
    psum x1 -> x0, waiting for transfers between devices: 121 us -> none  [local(): totals = lax.psum(joined.astype(jnp.bfloat16), 'tp').astype(jnp.float32)]
    all_gather x1 -> x0, waiting for transfers between devices: 64.3 us -> none  [local(): whole_acts = lax.all_gather(acts, 'tp', axis=1, tiled=True)]
    convert_element_type x0 -> x18, other arithmetic: none -> 42.6 us  [add(): return (a.astype(F32) + b.astype(F32)).astype(BF16)]
    ppermute x0 -> x22, starting transfers between devices: none -> 29.8 us  [the longest x10 19.4 us: local(): line = add(line, lax.ppermute(line, 'seq', pairs))]
    dot_general x5 -> x13, matrix products: 80.7 us -> 100 us  [the longest x4 32 us: local(): jnp.dot(teacher, proj_weight[:, cols], preferred_element_type=F32)]
    squeeze x0 -> x8, local copies, waits for them, and re-layouts: none -> 14.6 us  [the longest x4 9.87 us: local(): send = lax.dynamic_index_in_dim(terms, 1 - core, 1, keepdims=False)]
  transfers between devices with their start and end apart: 4 -> 22, of which waited for: 4 -> 8; matrix products, arithmetic and copies ran while one was open for 6% -> 29% of each run, Pallas kernels for 0% -> 0%
where the time goes in v1:
time: 523 us; the launch traced here: 514 us
  waiting for transfers between devices  308 us (59%)
  matrix products  100 us (19%)
  other arithmetic  50.7 us (10%)
  starting transfers between devices  29.8 us (6%)
  local copies, waits for them, and re-layouts  23.7 us (5%)
    ppermute x4, waiting for transfers between devices, local(): line = add(keep, lax.ppermute(send, 'seq', x_pairs))  158 us
    ppermute x10, waiting for transfers between devices, local(): line = add(line, lax.ppermute(line, 'seq', pairs))  120 us
    convert_element_type x18, other arithmetic, add(): return (a.astype(F32) + b.astype(F32)).astype(BF16)  42.6 us
    dot_general x4, matrix products, local(): jnp.dot(teacher, proj_weight[:, cols], preferred_element_type=F32)  32 us
    ppermute x4, waiting for transfers between devices, local(): other = lax.ppermute(part, 'tp', [(0, 1), (1, 0)])  30.4 us
    dot_general x4, matrix products, local(): lax.dot_general(resid[k], both, (((0,), (0,)), ((), ())), preferred_eleme...  29.2 us
    dot_general x4, matrix products, local(): jnp.dot(attn, out_weight[:, cols], preferred_element_type=F32)  23.2 us
    ppermute x10, starting transfers between devices, local(): line = add(line, lax.ppermute(line, 'seq', pairs))  19.4 us
  transfers between devices with their start and end apart: 22, of which 8 were waited for; matrix products, arithmetic and copies ran while one was open for 29% of the time, Pallas kernels for 0%

profile of v1, /device:TPU:0, one launch (start us, length us, event | category | flops | bytes accessed | tf_op | source)
XLA Modules:
  0.0 513.9 jit_solution(5690501269206774024)
XLA Ops:
  0.7 6.0 %fusion.14 = f32[512,1152]{1,0:T(8,128)S(1)} fusion(bf16[512,2048]{1,0:T(8,128)(2,1)} %param.6, bf16[2048,4608]{1,0:T(8,128)(2,1)} %param.8), kind=kOutput, calls=%fused_computation.22 | convolution fusion | flops 2415919104 | bytes 9175040 | tf_op jit(solution)/shard_map/dot_general | solution.py:61
  6.7 5.9 %fusion.62 = bf16[512,1152]{1,0:T(8,128)(2,1)} fusion(f32[512,1152]{1,0:T(8,128)S(1)} %fusion.14, bf16[512,1792]{1,0:T(8,128)(2,1)S(1)} %copy-done.3, bf16[1792,4608]{1,0:T(8,128)(2,1)} %param.9, pred[]{:T(512)S(6)} %eq.21, bf16[512,2304]{1,0:T(8,128)(2,1)S(1)} %copy-done.6), kind=kOutput, calls=%fused_computation.69 | convolution fusion | flops 2116878336 | bytes 10682369 | tf_op jit(solution)/shard_map/dot_general | solution.py:61
  12.6 3.0 collective-permute-start.2
  15.5 6.6 %fusion.16 = f32[512,1152]{1,0:T(8,128)} fusion(bf16[512,2048]{1,0:T(8,128)(2,1)S(1)} %copy-done.8, bf16[2048,4608]{1,0:T(8,128)(2,1)} %param.8), kind=kOutput, calls=%fused_computation.24 | convolution fusion | flops 2415919104 | bytes 9175040 | tf_op jit(solution)/shard_map/dot_general | solution.py:61
  22.2 6.9 %fusion.59 = bf16[512,1152]{1,0:T(8,128)(2,1)} fusion(f32[512,1152]{1,0:T(8,128)} %fusion.16, bf16[512,1792]{1,0:T(8,128)(2,1)S(1)} %copy-done.3, bf16[1792,4608]{1,0:T(8,128)(2,1)} %param.9, pred[]{:T(512)S(6)} %eq.20, bf16[512,2304]{1,0:T(8,128)(2,1)} %param.5), kind=kOutput, calls=%fused_computation.68 | convolution fusion | flops 2116878336 | bytes 10682369 | tf_op jit(solution)/shard_map/dot_general | solution.py:61
  29.1 5.4 %fusion.18 = f32[512,1152]{1,0:T(8,128)S(1)} fusion(bf16[512,2048]{1,0:T(8,128)(2,1)S(1)} %copy-done.9, bf16[2048,4608]{1,0:T(8,128)(2,1)} %param.8), kind=kOutput, calls=%fused_computation.26 | convolution fusion | flops 2415919104 | bytes 9175040 | tf_op jit(solution)/shard_map/dot_general | solution.py:61
  34.5 15.7 %fusion.56 = bf16[512,1152]{1,0:T(8,128)(2,1)S(1)} fusion(f32[512,1152]{1,0:T(8,128)S(1)} %fusion.18, bf16[512,1792]{1,0:T(8,128)(2,1)S(1)} %copy-done.3, bf16[1792,4608]{1,0:T(8,128)(2,1)S(1)} %bitcast.76, pred[]{:T(512)S(6)} %eq.20, bf16[512,2304]{1,0:T(8,128)(2,1)S(1)} %copy-done.7), kind=kOutput, calls=%fused_computation.67 | convolution fusion | flops 2116878336 | bytes 10682369 | tf_op jit(solution)/shard_map/dot_general | solution.py:61
  50.2 1.9 collective-permute-start
  52.1 5.2 %fusion.12 = f32[512,1152]{1,0:T(8,128)S(1)} fusion(bf16[512,2048]{1,0:T(8,128)(2,1)S(1)} %copy-done.9, bf16[2048,4608]{1,0:T(8,128)(2,1)} %param.8), kind=kOutput, calls=%fused_computation.20 | convolution fusion | flops 2415919104 | bytes 9175040 | tf_op jit(solution)/shard_map/dot_general | solution.py:61
  57.3 3.6 fusion.65
  61.3 1.5 neg.3
  62.8 30.4 %collective-permute-done = bf16[512,1152]{1,0:T(8,128)(2,1)} collective-permute-done((bf16[512,1152]{1,0:T(8,128)(2,1)S(1)}, bf16[512,1152]{1,0:T(8,128)(2,1)}, u32[]{:S(2)}, u32[]{:S(2)}) %collective-permute-start) | collective-permute-done | bytes 1179680 | tf_op jit(solution)/shard_map/ppermute | solution.py:67
  93.2 1.9 add_convert_fusion.13
  95.1 6.8 %convolution_convert_fusion = bf16[1152,3840]{1,0:T(8,128)(2,1)S(1)} fusion(bf16[512,1152]{1,0:T(8,128)(2,1)S(1)} %add_convert_fusion.13, bf16[512,1792]{1,0:T(8,128)(2,1)S(1)} %copy-done.4, bf16[512,2048]{1,0:T(8,128)(2,1)} %param.6), kind=kOutput, calls=%fused_computation | convolution fusion | flops 4542136320 | bytes 13959168 | tf_op jit(solution)/shard_map/dot_general | solution.py:71
  102.0 2.3 dynamic-slice_bitcast_fusion
  104.3 3.0 add_convert_fusion.12
  107.2 7.3 %convolution_convert_fusion.2 = bf16[1152,3840]{1,0:T(8,128)(2,1)S(1)} fusion(bf16[512,1152]{1,0:T(8,128)(2,1)} %add_convert_fusion.12, bf16[512,1792]{1,0:T(8,128)(2,1)} %neg.3, bf16[512,2048]{1,0:T(8,128)(2,1)} %param.6), kind=kOutput, calls=%fused_computation.2 | convolution fusion | flops 4542136320 | bytes 13959168 | tf_op jit(solution)/shard_map/dot_general | solution.py:71
  114.6 2.6 dynamic-slice_bitcast_fusion.2
  117.1 2.3 copy-done.1
  119.9 2.9 add_convert_fusion.10
  122.8 7.3 %convolution_convert_fusion.1 = bf16[1152,3840]{1,0:T(8,128)(2,1)S(1)} fusion(bf16[512,1152]{1,0:T(8,128)(2,1)} %add_convert_fusion.10, bf16[512,1792]{1,0:T(8,128)(2,1)} %neg.3, bf16[512,2048]{1,0:T(8,128)(2,1)} %param.6), kind=kOutput, calls=%fused_computation.1 | convolution fusion | flops 4542136320 | bytes 13959168 | tf_op jit(solution)/shard_map/dot_general | solution.py:71
  130.1 2.5 dynamic-slice_bitcast_fusion.1
  132.6 2.3 copy-done.2
  135.0 2.9 add_convert_fusion.11
  137.9 7.7 %convolution_convert_fusion.3 = bf16[1152,3840]{1,0:T(8,128)(2,1)S(1)} fusion(bf16[512,1152]{1,0:T(8,128)(2,1)} %add_convert_fusion.11, bf16[512,1792]{1,0:T(8,128)(2,1)} %neg.3, bf16[512,2048]{1,0:T(8,128)(2,1)} %param.6), kind=kOutput, calls=%fused_computation.3 | convolution fusion | flops 4542136320 | bytes 13959168 | tf_op jit(solution)/shard_map/dot_general | solution.py:71
  145.7 2.5 dynamic-slice_bitcast_fusion.3
  148.2 2.2 copy-done
  150.9 3.4 fusion
  154.3 1.5 dynamic-slice_bitcast_fusion.4
  155.8 2.0 collective-permute-start.18
  157.9 4.6 fusion.2
  162.5 1.6 dynamic-slice_bitcast_fusion.6
  164.1 4.6 fusion.1
  168.7 1.5 dynamic-slice_bitcast_fusion.5
  170.2 2.0 collective-permute-start.13
  172.2 4.6 fusion.3
  177.1 30.0 %collective-permute-done.18 = bf16[288,3840]{1,0:T(8,128)(2,1)} collective-permute-done((bf16[288,3840]{1,0:T(8,128)(2,1)}, bf16[288,3840]{1,0:T(8,128)(2,1)}, u32[]{:S(2)}, u32[]{:S(2)}) %collective-permute-start.18) | collective-permute-done | bytes 2211872 | tf_op jit(solution)/shard_map/ppermute | solution.py:80
  207.1 2.2 fusion.20
  209.3 0.8 collective-permute-start.19
  210.1 91.8 %collective-permute-done.13 = bf16[288,3840]{1,0:T(8,128)(2,1)} collective-permute-done((bf16[288,3840]{1,0:T(8,128)(2,1)}, bf16[288,3840]{1,0:T(8,128)(2,1)}, u32[]{:S(2)}, u32[]{:S(2)}) %collective-permute-start.13) | collective-permute-done | bytes 2211872 | tf_op jit(solution)/shard_map/ppermute | solution.py:80
  301.9 2.2 fusion.21
  304.1 4.2 collective-permute-start.14
  308.3 2.2 fusion.22
  310.5 1.6 collective-permute-start.10
  312.1 36.4 %collective-permute-done.5 = bf16[288,3840]{1,0:T(8,128)(2,1)S(1)} collective-permute-done((bf16[288,3840]{1,0:T(8,128)(2,1)S(1)}, bf16[288,3840]{1,0:T(8,128)(2,1)S(1)}, u32[]{:S(2)}, u32[]{:S(2)}) %collective-permute-start.5) | collective-permute-done | bytes 2211872 | tf_op jit(solution)/shard_map/ppermute | solution.py:80
  348.5 0.6 fusion.23
  349.1 3.9 collective-permute-start.6
  353.5 0.8 collective-permute-start.20
  354.3 2.3 collective-permute-done.14
  357.2 0.8 collective-permute-start.15
  358.0 46.1 %collective-permute-done.10 = bf16[288,3840]{1,0:T(8,128)(2,1)S(1)} collective-permute-done((bf16[288,3840]{1,0:T(8,128)(2,1)S(1)}, bf16[288,3840]{1,0:T(8,128)(2,1)S(1)}, u32[]{:S(2)}, u32[]{:S(2)}) %collective-permute-start.10) | collective-permute-done | bytes 2211872 | tf_op jit(solution)/shard_map/ppermute | solution.py:83
  404.6 2.1 collective-permute-start.11
  406.6 42.0 %collective-permute-done.6 = bf16[288,3840]{1,0:T(8,128)(2,1)S(1)} collective-permute-done((bf16[288,3840]{1,0:T(8,128)(2,1)S(1)}, bf16[288,3840]{1,0:T(8,128)(2,1)S(1)}, u32[]{:S(2)}, u32[]{:S(2)}) %collective-permute-start.6) | collective-permute-done | bytes 2211872 | tf_op jit(solution)/shard_map/ppermute | solution.py:83
  448.6 1.9 add_convert_fusion.9
  450.6 2.0 collective-permute-start.7
  452.6 2.0 add_convert_fusion.1
  454.6 1.3 collective-permute-start.21
  455.9 1.9 add_convert_fusion.4
  457.8 2.0 collective-permute-start.16
  459.8 15.7 %fusion.68 = bf16[512,2048]{1,0:T(8,128)(2,1)} fusion(bf16[2048,4608]{1,0:T(8,128)(2,1)} %param.8, bf16[512,1152]{1,0:T(8,128)(2,1)} %add_convert_fusion.10, bf16[512,1152]{1,0:T(8,128)(2,1)} %add_convert_fusion.11, bf16[512,1152]{1,0:T(8,128)(2,1)} %add_convert_fusion.12, bf16[512,1152]{1,0:T(8,128)(2,1)S(1)} %add_convert_fusion.13), kind=kOutput, calls=%fused_computation.71 | convolution fusion | flops 9683599360 | bytes 25690112 | tf_op jit(solution)/shard_map/dot_general | solution.py:86
  475.6 29.4 %collective-permute-done.21 = bf16[288,3840]{1,0:T(8,128)(2,1)} collective-permute-done((bf16[288,3840]{1,0:T(8,128)(2,1)}, bf16[288,3840]{1,0:T(8,128)(2,1)}, u32[]{:S(2)}, u32[]{:S(2)}) %collective-permute-start.21) | collective-permute-done | bytes 2211872 | tf_op jit(solution)/shard_map/ppermute | solution.py:83
  504.9 6.6 %fusion.72 = bf16[3840,288]{0,1:T(8,128)(2,1)S(1)} fusion(bf16[288,3840]{1,0:T(8,128)(2,1)} %collective-permute-done.7, bf16[288,3840]{1,0:T(8,128)(2,1)} %add_convert_fusion.9, bf16[288,3840]{1,0:T(8,128)(2,1)} %collective-permute-done.11, bf16[288,3840]{1,0:T(8,128)(2,1)S(1)} %add_convert_fusion.7, bf16[288,3840]{1,0:T(8,128)(2,1)} %collective-permute-done.16, ...), kind=kLoop, calls=%fused_computation.81 | loop fusion | flops 21012480 | bytes 19906564 | tf_op jit(solution)/shard_map/transpose | solution.py:89
  511.5 1.0 slice.51
  512.5 1.2 slice.50
  (52 shorter events, 3.2 us)
Async XLA Ops:
  0.6 6.0 %copy-start.3 = (bf16[512,1792]{1,0:T(8,128)(2,1)S(1)}, bf16[512,1792]{1,0:T(8,128)(2,1)}, u32[]{:S(2)}) copy-start(bf16[512,1792]{1,0:T(8,128)(2,1)} %param.7) | copy-start | bytes 5505028
  0.6 6.0 %copy-start.6 = (bf16[512,2304]{1,0:T(8,128)(2,1)S(1)}, bf16[512,2304]{1,0:T(8,128)(2,1)}, u32[]{:S(2)}) copy-start(bf16[512,2304]{1,0:T(8,128)(2,1)} %param.5) | copy-start | bytes 7077892
  6.7 8.9 %copy-start.8 = (bf16[512,2048]{1,0:T(8,128)(2,1)S(1)}, bf16[512,2048]{1,0:T(8,128)(2,1)}, u32[]{:S(2)}) copy-start(bf16[512,2048]{1,0:T(8,128)(2,1)} %param.6) | copy-start | bytes 6291460
  12.6 122.4 %collective-permute-start.2 = (bf16[512,1152]{1,0:T(8,128)(2,1)}, bf16[512,1152]{1,0:T(8,128)(2,1)}, u32[]{:S(2)}, u32[]{:S(2)}) collective-permute-start(bf16[512,1152]{1,0:T(8,128)(2,1)} %fusion.62), channel_id=1, source_target_pairs={{0,1},{1,0},{2,3},{3,2},{4,5},{5,4},{6,7},{7,6},{8,9},{9,8},{10,11... | collective-permute-start | bytes 3538952 | tf_op jit(solution)/shard_map/ppermute | solution.py:67
  22.2 6.9 %copy-start.9 = (bf16[512,2048]{1,0:T(8,128)(2,1)S(1)}, bf16[512,2048]{1,0:T(8,128)(2,1)}, u32[]{:S(2)}) copy-start(bf16[512,2048]{1,0:T(8,128)(2,1)} %param.6) | copy-start | bytes 6291460
  22.2 12.3 %slice-start = ((s8[16515072]{0:T(1024)(128)(4,1)}), s8[4194304]{0:T(1024)(128)(4,1)S(1)}, s32[]{:S(2)}) async-start(s8[16515072]{0:T(1024)(128)(4,1)} %bitcast.75), calls=%async_computation | async-start | bytes 8388608
  22.2 12.3 %slice-start.1 = ((s8[16515072]{0:T(1024)(128)(4,1)}), s8[4194304]{0:T(1024)(128)(4,1)S(1)}, s32[]{:S(2)}) async-start(s8[16515072]{0:T(1024)(128)(4,1)} %bitcast.75), calls=%async_computation.1 | async-start | bytes 8388608
  22.2 12.3 %slice-start.2 = ((s8[16515072]{0:T(1024)(128)(4,1)}), s8[4194304]{0:T(1024)(128)(4,1)S(1)}, s32[]{:S(2)}) async-start(s8[16515072]{0:T(1024)(128)(4,1)} %bitcast.75), calls=%async_computation.2 | async-start | bytes 8388608
  29.1 5.4 %slice-start.3 = ((s8[16515072]{0:T(1024)(128)(4,1)}), s8[3932160]{0:T(1024)(128)(4,1)S(1)}, s32[]{:S(2)}) async-start(s8[16515072]{0:T(1024)(128)(4,1)} %bitcast.75), calls=%async_computation.3 | async-start | bytes 7864320
  29.1 5.4 %copy-start.7 = (bf16[512,2304]{1,0:T(8,128)(2,1)S(1)}, bf16[512,2304]{1,0:T(8,128)(2,1)}, u32[]{:S(2)}) copy-start(bf16[512,2304]{1,0:T(8,128)(2,1)} %param.5) | copy-start | bytes 7077892
  29.1 75.2 %collective-permute-start.1 = (bf16[512,1152]{1,0:T(8,128)(2,1)}, bf16[512,1152]{1,0:T(8,128)(2,1)}, u32[]{:S(2)}, u32[]{:S(2)}) collective-permute-start(bf16[512,1152]{1,0:T(8,128)(2,1)} %fusion.59), channel_id=1, source_target_pairs={{0,1},{1,0},{2,3},{3,2},{4,5},{5,4},{6,7},{7,6},{8,9},{9,8},{10,11... | collective-permute-start | bytes 3538952 | tf_op jit(solution)/shard_map/ppermute | solution.py:67
  50.2 7.1 %copy-start.5 = (bf16[512,1152]{1,0:T(8,128)(2,1)}, bf16[512,1152]{1,0:T(8,128)(2,1)S(1)}, u32[]{:S(2)}) copy-start(bf16[512,1152]{1,0:T(8,128)(2,1)S(1)} %fusion.56) | copy-start | bytes 3538948
  50.2 43.0 %collective-permute-start = (bf16[512,1152]{1,0:T(8,128)(2,1)S(1)}, bf16[512,1152]{1,0:T(8,128)(2,1)}, u32[]{:S(2)}, u32[]{:S(2)}) collective-permute-start(bf16[512,1152]{1,0:T(8,128)(2,1)S(1)} %fusion.56), channel_id=1, source_target_pairs={{0,1},{1,0},{2,3},{3,2},{4,5},{5,4},{6,7},{7,6},{8,9},{9,8},{10,11... | collective-permute-start | bytes 3538952 | tf_op jit(solution)/shard_map/ppermute | solution.py:67
  60.9 59.0 %collective-permute-start.3 = (bf16[512,1152]{1,0:T(8,128)(2,1)}, bf16[512,1152]{1,0:T(8,128)(2,1)}, u32[]{:S(2)}, u32[]{:S(2)}) collective-permute-start(bf16[512,1152]{1,0:T(8,128)(2,1)} %fusion.65), channel_id=1, source_target_pairs={{0,1},{1,0},{2,3},{3,2},{4,5},{5,4},{6,7},{7,6},{8,9},{9,8},{10,11... | collective-permute-start | bytes 3538952 | tf_op jit(solution)/shard_map/ppermute | solution.py:67
  62.8 32.3 %copy-start.4 = (bf16[512,1792]{1,0:T(8,128)(2,1)S(1)}, bf16[512,1792]{1,0:T(8,128)(2,1)}, u32[]{:S(2)}) copy-start(bf16[512,1792]{1,0:T(8,128)(2,1)} %neg.3) | copy-start | bytes 5505028
  104.3 46.7 %collective-permute-start.17 = (bf16[2,288,3840]{2,1,0:T(8,128)(2,1)}, bf16[2,288,3840]{2,1,0:T(8,128)(2,1)}, u32[]{:S(2)}, u32[]{:S(2)}) collective-permute-start(bf16[2,288,3840]{2,1,0:T(8,128)(2,1)} %dynamic-slice_bitcast_fusion), channel_id=1, source_target_pairs={{0,2},{2,0},{4,6},{6,4},{8,10},{10,8},{12,14},{14,12},{16,18},{18,... | collective-permute-start | bytes 13271048 | tf_op jit(solution)/shard_map/ppermute | solution.py:77
  114.5 4.8 copy-start.1
  119.4 38.5 %collective-permute-start.8 = (bf16[2,288,3840]{2,1,0:T(8,128)(2,1)}, bf16[2,288,3840]{2,1,0:T(8,128)(2,1)}, u32[]{:S(2)}, u32[]{:S(2)}) collective-permute-start(bf16[2,288,3840]{2,1,0:T(8,128)(2,1)} %dynamic-slice_bitcast_fusion.2), channel_id=1, source_target_pairs={{0,2},{2,0},{4,6},{6,4},{8,10},{10,8},{12,14},{14,12},{16,18},{18,... | collective-permute-start | bytes 13271048 | tf_op jit(solution)/shard_map/ppermute | solution.py:77
  130.1 4.8 copy-start.2
  135.0 29.1 %collective-permute-start.12 = (bf16[2,288,3840]{2,1,0:T(8,128)(2,1)}, bf16[2,288,3840]{2,1,0:T(8,128)(2,1)}, u32[]{:S(2)}, u32[]{:S(2)}) collective-permute-start(bf16[2,288,3840]{2,1,0:T(8,128)(2,1)} %dynamic-slice_bitcast_fusion.1), channel_id=1, source_target_pairs={{0,2},{2,0},{4,6},{6,4},{8,10},{10,8},{12,14},{14,12},{16,18},{18,... | collective-permute-start | bytes 13271048 | tf_op jit(solution)/shard_map/ppermute | solution.py:77
  145.7 4.8 copy-start
  150.4 21.8 %collective-permute-start.4 = (bf16[2,288,3840]{2,1,0:T(8,128)(2,1)}, bf16[2,288,3840]{2,1,0:T(8,128)(2,1)}, u32[]{:S(2)}, u32[]{:S(2)}) collective-permute-start(bf16[2,288,3840]{2,1,0:T(8,128)(2,1)} %dynamic-slice_bitcast_fusion.3), channel_id=1, source_target_pairs={{0,2},{2,0},{4,6},{6,4},{8,10},{10,8},{12,14},{14,12},{16,18},{18,... | collective-permute-start | bytes 13271048 | tf_op jit(solution)/shard_map/ppermute | solution.py:77
  155.8 51.2 %collective-permute-start.18 = (bf16[288,3840]{1,0:T(8,128)(2,1)}, bf16[288,3840]{1,0:T(8,128)(2,1)}, u32[]{:S(2)}, u32[]{:S(2)}) collective-permute-start(bf16[288,3840]{1,0:T(8,128)(2,1)} %dynamic-slice_bitcast_fusion.4), channel_id=1, source_target_pairs={{0,4},{2,6},{4,0},{6,2},{8,12},{10,14},{12,8},{14,10},{16,20},{18,... | collective-permute-start | bytes 6635528 | tf_op jit(solution)/shard_map/ppermute | solution.py:80
  164.1 144.2 %collective-permute-start.9 = (bf16[288,3840]{1,0:T(8,128)(2,1)}, bf16[288,3840]{1,0:T(8,128)(2,1)}, u32[]{:S(2)}, u32[]{:S(2)}) collective-permute-start(bf16[288,3840]{1,0:T(8,128)(2,1)} %dynamic-slice_bitcast_fusion.6), channel_id=1, source_target_pairs={{0,4},{2,6},{4,0},{6,2},{8,12},{10,14},{12,8},{14,10},{16,20},{18,... | collective-permute-start | bytes 6635528 | tf_op jit(solution)/shard_map/ppermute | solution.py:80
  170.2 131.7 %collective-permute-start.13 = (bf16[288,3840]{1,0:T(8,128)(2,1)}, bf16[288,3840]{1,0:T(8,128)(2,1)}, u32[]{:S(2)}, u32[]{:S(2)}) collective-permute-start(bf16[288,3840]{1,0:T(8,128)(2,1)} %dynamic-slice_bitcast_fusion.5), channel_id=1, source_target_pairs={{0,4},{2,6},{4,0},{6,2},{8,12},{10,14},{12,8},{14,10},{16,20},{18,... | collective-permute-start | bytes 6635528 | tf_op jit(solution)/shard_map/ppermute | solution.py:80
  177.0 171.5 %collective-permute-start.5 = (bf16[288,3840]{1,0:T(8,128)(2,1)S(1)}, bf16[288,3840]{1,0:T(8,128)(2,1)S(1)}, u32[]{:S(2)}, u32[]{:S(2)}) collective-permute-start(bf16[288,3840]{1,0:T(8,128)(2,1)S(1)} %dynamic-slice_bitcast_fusion.7), channel_id=1, source_target_pairs={{0,4},{2,6},{4,0},{6,2},{8,12},{10,14},{12,8},{14,10},{16,20},{18,... | collective-permute-start | bytes 6635528 | tf_op jit(solution)/shard_map/ppermute | solution.py:80
  209.3 143.7 %collective-permute-start.19 = (bf16[288,3840]{1,0:T(8,128)(2,1)S(1)}, bf16[288,3840]{1,0:T(8,128)(2,1)S(1)}, u32[]{:S(2)}, u32[]{:S(2)}) collective-permute-start(bf16[288,3840]{1,0:T(8,128)(2,1)S(1)} %fusion.20), channel_id=1, source_target_pairs={{24,16},{26,18},{28,20},{30,22},{25,17},{27,19},{29,21},{31,23}} | collective-permute-start | bytes 6635528 | tf_op jit(solution)/shard_map/ppermute | solution.py:83
  304.1 52.6 %collective-permute-start.14 = (bf16[288,3840]{1,0:T(8,128)(2,1)S(1)}, bf16[288,3840]{1,0:T(8,128)(2,1)S(1)}, u32[]{:S(2)}, u32[]{:S(2)}) collective-permute-start(bf16[288,3840]{1,0:T(8,128)(2,1)S(1)} %fusion.21), channel_id=1, source_target_pairs={{0,8},{2,10},{4,12},{6,14},{1,9},{3,11},{5,13},{7,15}} | collective-permute-start | bytes 6635528 | tf_op jit(solution)/shard_map/ppermute | solution.py:83
  310.5 93.6 %collective-permute-start.10 = (bf16[288,3840]{1,0:T(8,128)(2,1)S(1)}, bf16[288,3840]{1,0:T(8,128)(2,1)S(1)}, u32[]{:S(2)}, u32[]{:S(2)}) collective-permute-start(bf16[288,3840]{1,0:T(8,128)(2,1)S(1)} %fusion.22), channel_id=1, source_target_pairs={{24,16},{26,18},{28,20},{30,22},{0,8},{2,10},{4,12},{6,14},{25,17}... | collective-permute-start | bytes 6635528 | tf_op jit(solution)/shard_map/ppermute | solution.py:83
  349.1 99.5 %collective-permute-start.6 = (bf16[288,3840]{1,0:T(8,128)(2,1)S(1)}, bf16[288,3840]{1,0:T(8,128)(2,1)S(1)}, u32[]{:S(2)}, u32[]{:S(2)}) collective-permute-start(bf16[288,3840]{1,0:T(8,128)(2,1)S(1)} %fusion.23), channel_id=1, source_target_pairs={{0,8},{2,10},{4,12},{6,14},{24,16},{26,18},{28,20},{30,22},{1,9},{... | collective-permute-start | bytes 6635528 | tf_op jit(solution)/shard_map/ppermute | solution.py:83
  353.5 99.1 %collective-permute-start.20 = (bf16[288,3840]{1,0:T(8,128)(2,1)S(1)}, bf16[288,3840]{1,0:T(8,128)(2,1)S(1)}, u32[]{:S(2)}, u32[]{:S(2)}) collective-permute-start(bf16[288,3840]{1,0:T(8,128)(2,1)S(1)} %add_convert_fusion.2), channel_id=1, source_target_pairs={{16,8},{18,10},{20,12},{22,14},{17,9},{19,11},{21,13},{23,15}} | collective-permute-start | bytes 6635528 | tf_op jit(solution)/shard_map/ppermute | solution.py:83
  357.2 98.7 %collective-permute-start.15 = (bf16[288,3840]{1,0:T(8,128)(2,1)S(1)}, bf16[288,3840]{1,0:T(8,128)(2,1)S(1)}, u32[]{:S(2)}, u32[]{:S(2)}) collective-permute-start(bf16[288,3840]{1,0:T(8,128)(2,1)S(1)} %add_convert_fusion.5), channel_id=1, source_target_pairs={{8,16},{10,18},{12,20},{14,22},{9,17},{11,19},{13,21},{15,23}} | collective-permute-start | bytes 6635528 | tf_op jit(solution)/shard_map/ppermute | solution.py:83
  404.6 71.0 %collective-permute-start.11 = (bf16[288,3840]{1,0:T(8,128)(2,1)S(1)}, bf16[288,3840]{1,0:T(8,128)(2,1)}, u32[]{:S(2)}, u32[]{:S(2)}) collective-permute-start(bf16[288,3840]{1,0:T(8,128)(2,1)S(1)} %add_convert_fusion.7), channel_id=1, source_target_pairs={{16,8},{18,10},{20,12},{22,14},{17,9},{19,11},{21,13},{23,15}} | collective-permute-start | bytes 6635528 | tf_op jit(solution)/shard_map/ppermute | solution.py:83
  450.6 25.0 %collective-permute-start.7 = (bf16[288,3840]{1,0:T(8,128)(2,1)}, bf16[288,3840]{1,0:T(8,128)(2,1)}, u32[]{:S(2)}, u32[]{:S(2)}) collective-permute-start(bf16[288,3840]{1,0:T(8,128)(2,1)} %add_convert_fusion.9), channel_id=1, source_target_pairs={{8,16},{10,18},{12,20},{14,22},{9,17},{11,19},{13,21},{15,23}} | collective-permute-start | bytes 6635528 | tf_op jit(solution)/shard_map/ppermute | solution.py:83
  454.6 50.3 %collective-permute-start.21 = (bf16[288,3840]{1,0:T(8,128)(2,1)}, bf16[288,3840]{1,0:T(8,128)(2,1)}, u32[]{:S(2)}, u32[]{:S(2)}) collective-permute-start(bf16[288,3840]{1,0:T(8,128)(2,1)} %add_convert_fusion.1), channel_id=1, source_target_pairs={{8,0},{10,2},{12,4},{14,6},{9,1},{11,3},{13,5},{15,7}} | collective-permute-start | bytes 6635528 | tf_op jit(solution)/shard_map/ppermute | solution.py:83
  457.8 47.1 %collective-permute-start.16 = (bf16[288,3840]{1,0:T(8,128)(2,1)}, bf16[288,3840]{1,0:T(8,128)(2,1)}, u32[]{:S(2)}, u32[]{:S(2)}) collective-permute-start(bf16[288,3840]{1,0:T(8,128)(2,1)} %add_convert_fusion.4), channel_id=1, source_target_pairs={{16,24},{18,26},{20,28},{22,30},{17,25},{19,27},{21,29},{23,31}} | collective-permute-start | bytes 6635528 | tf_op jit(solution)/shard_map/ppermute | solution.py:83

commit v2 on v1

v2 whole, which is shorter than its diff:
```python
import functools

import jax
import jax.numpy as jnp
from jax import lax
from jax.sharding import PartitionSpec as P

F32 = jnp.float32
BF16 = jnp.bfloat16


def generic(acts, attn, teacher, out_weight, proj_weight):
    joined = jnp.dot(attn, out_weight, preferred_element_type=F32) - jnp.dot(
        teacher, proj_weight, preferred_element_type=F32
    )
    totals = lax.psum(joined.astype(BF16), "tp").astype(F32)
    whole_acts = lax.all_gather(acts, "tp", axis=1, tiled=True)
    resid_grad = (whole_acts.astype(F32) + totals).astype(BF16)
    attn_grad = lax.dot_general(
        resid_grad, out_weight, (((1,), (1,)), ((), ())), preferred_element_type=F32
    ).astype(BF16)
    out_terms = lax.dot_general(
        attn, resid_grad, (((0,), (0,)), ((), ())), preferred_element_type=F32
    )
    proj_terms = -lax.dot_general(
        teacher, resid_grad, (((0,), (0,)), ((), ())), preferred_element_type=F32
    )
    return (
        attn_grad,
        lax.psum_scatter(out_terms.astype(BF16), "seq", scatter_dimension=1, tiled=True),
        lax.psum_scatter(proj_terms.astype(BF16), "seq", scatter_dimension=1, tiled=True),
    )


def add(a, b):
    return (a.astype(F32) + b.astype(F32)).astype(BF16)


def after(value, *needs):
    return lax.optimization_barrier((value,) + needs)[0]


def local(acts, attn, teacher, out_weight, proj_weight):
    s = lax.axis_index("seq")
    tp = lax.axis_index("tp")
    core, x, z = s % 2, (s // 2) % 2, s // 4
    width = out_weight.shape[1] // 4
    strip = width // 4
    half = acts.shape[1]
    core_pairs = [(i, i ^ 1) for i in range(16)]
    x_pairs = [(i, i ^ 2) for i in range(16)]
    hops = {
        0: [[(3, 2)], [(2, 1)], [(1, 0)]],
        1: [[(3, 2), (0, 1)], [(2, 1)]],
        2: [[(0, 1), (3, 2)], [(1, 2)]],
        3: [[(0, 1)], [(1, 2)], [(2, 3)]],
    }
    order = [0, 3, 1, 2]

    def partial(k, *needs):
        cols = slice(k * width, (k + 1) * width)
        a, t = (after(attn, *needs), after(teacher, *needs)) if needs else (attn, teacher)
        part = jnp.dot(a, out_weight[:, cols], preferred_element_type=F32) - jnp.dot(
            t, proj_weight[:, cols], preferred_element_type=F32
        )
        own, at = divmod(k * width, half)
        mine = jnp.where(tp == own, acts[:, at : at + width].astype(F32), 0.0)
        return (part + mine).astype(BF16)

    def over_tp(part):
        return add(part, lax.ppermute(part, "tp", [(0, 1), (1, 0)]))

    def terms(grad, features, sign):
        value = sign * lax.dot_general(
            grad, features, (((0,), (0,)), ((), ())), preferred_element_type=F32
        )
        value = value.astype(BF16).reshape(2, 2, strip, -1)
        keep = lax.dynamic_index_in_dim(value, core, 1, keepdims=False)
        send = lax.dynamic_index_in_dim(value, 1 - core, 1, keepdims=False)
        return keep, send

    resid, chip, line = {}, {}, {}
    hop_done = {}
    parts = {0: partial(order[0]), 1: None}
    parts[1] = partial(order[1])
    resid[0] = over_tp(parts[0])
    pieces = []
    attn_grad = None

    def advance(n, stage):
        if n < 0:
            return None
        steps = hops[order[n // 2]]
        if stage >= len(steps):
            return None
        pairs = [(a * 4 + i, b * 4 + i) for a, b in steps[stage] for i in range(4)]
        line[n] = add(line[n], lax.ppermute(line[n], "seq", pairs))
        return line[n]

    for i in range(4):
        keep_send = [terms(resid[i], attn, 1.0), terms(resid[i], teacher, -1.0)]
        if i + 1 < 4:
            resid[i + 1] = over_tp(after(parts[i + 1], resid[i]))
        if i + 2 < 4:
            parts[i + 2] = partial(order[i + 2], keep_send[0][1], keep_send[1][1])
        for j in range(2):
            n = 2 * i + j
            keep, send = keep_send[j]
            chip[n] = add(keep, lax.ppermute(send, "seq", core_pairs))
        if i == 3:
            whole = jnp.concatenate([resid[order.index(k)] for k in range(4)], axis=1)
            attn_grad = lax.dot_general(
                whole, out_weight, (((1,), (1,)), ((), ())), preferred_element_type=F32
            ).astype(BF16)
        for j in range(2):
            n = 2 * i + j
            needs = [line[n - 2]] if n >= 2 else []
            for back, stage in ((4, 0), (5, 1), (6, 2)):
                moved = advance(n - back, stage)
                if moved is not None:
                    needs.append(moved)
            if n == 7:
                needs.append(attn_grad)
            value = after(chip[n], *needs) if needs else chip[n]
            keep = lax.dynamic_index_in_dim(value, x, 0, keepdims=False)
            send = lax.dynamic_index_in_dim(value, 1 - x, 0, keepdims=False)
            line[n] = add(keep, lax.ppermute(send, "seq", x_pairs))
    for n in range(8, 14):
        for back, stage in ((4, 0), (5, 1), (6, 2)):
            if n - back < 8:
                advance(n - back, stage)
    grads = []
    for j in range(2):
        total = line[j]
        for i in range(1, 4):
            total = jnp.where(z == order[i], line[2 * i + j], total)
        grads.append(total.T)
    return attn_grad, grads[0], grads[1]


def solution(mesh):
    placed = (P("seq", "tp"), P("seq", "tp"), P("seq", "tp"), P("tp", None), P("tp", None))
    tuned = mesh.shape["seq"] == 16 and mesh.shape["tp"] == 2
    return jax.shard_map(
        local if tuned else generic,
        mesh=mesh,
        in_specs=placed,
        out_specs=(P("seq", "tp"), P("tp", "seq"), P("tp", "seq")),
        check_vma=False,
    )
```

time: 523 us -> 445 us (0.85)
  the two profiles are of different devices: /device:TPU:0 before, /device:TPU:20 now
where the time goes in v2:
time: 445 us; the launch traced here: 437 us
  waiting for transfers between devices  249 us (56%)
  matrix products  80.9 us (18%)
  starting transfers between devices  46.8 us (11%)
  other arithmetic  42 us (9%)
  local copies, waits for them, and re-layouts  16 us (4%)
    ppermute x20, waiting for transfers between devices, advance(): line[n] = add(line[n], lax.ppermute(line[n], 'seq', pairs))  119 us
    ppermute x4, waiting for transfers between devices, over_tp(): return add(part, lax.ppermute(part, 'tp', [(0, 1), (1, 0)]))  72.7 us
    ppermute x8, waiting for transfers between devices, local(): line[n] = add(keep, lax.ppermute(send, 'seq', x_pairs))  57.1 us
    ppermute x20, starting transfers between devices, advance(): line[n] = add(line[n], lax.ppermute(line[n], 'seq', pairs))  33.4 us
    convert_element_type x34, other arithmetic, add(): return (a.astype(F32) + b.astype(F32)).astype(BF16)  31.4 us
    dot_general x8, matrix products, terms(): lax.dot_general(grad, features, (((0,), (0,)), ((), ())), preferred_eleme...  24.9 us
    dot_general x4, matrix products, partial(): jnp.dot(a, out_weight[:, cols], preferred_element_type=F32)  21.4 us
    dot_general x4, matrix products, partial(): jnp.dot(t, proj_weight[:, cols], preferred_element_type=F32)  18.8 us
  transfers between devices with their start and end apart: 40, of which 17 were waited for; matrix products, arithmetic and copies ran while one was open for 25% of the time, Pallas kernels for 0%

profile of v2, /device:TPU:20, one launch (start us, length us, event | category | flops | bytes accessed | tf_op | source)
XLA Modules:
  0.0 436.5 jit_solution(7048627716277764932)
XLA Ops:
  0.7 1.6 copy-done
  2.2 5.4 %fusion.22 = f32[512,1152]{1,0:T(8,128)S(1)} fusion(bf16[512,2048]{1,0:T(8,128)(2,1)S(1)} %copy-done, bf16[2048,4608]{1,0:T(8,128)(2,1)} %param.8), kind=kOutput, calls=%fused_computation.34 | convolution fusion | flops 2415919104 | bytes 9175040 | tf_op jit(solution)/shard_map/dot_general | solution.py:63
  7.6 4.7 %fusion.60 = bf16[512,1152]{1,0:T(8,128)(2,1)S(1)} fusion(f32[512,1152]{1,0:T(8,128)S(1)} %fusion.22, bf16[512,1792]{1,0:T(8,128)(2,1)S(1)} %copy-done.22, bf16[1792,4608]{1,0:T(8,128)(2,1)} %param.9, pred[]{:T(512)S(6)} %eq.23, bf16[512,2304]{1,0:T(8,128)(2,1)S(1)} %copy-done.19), kind=kOutput, calls=%fused_computation.60 | convolution fusion | flops 2116878336 | bytes 10682369 | tf_op jit(solution)/shard_map/dot_general | solution.py:63
  12.9 5.3 %fusion.18 = f32[512,1152]{1,0:T(8,128)S(1)} fusion(bf16[512,2048]{1,0:T(8,128)(2,1)S(1)} %copy-done, bf16[2048,4608]{1,0:T(8,128)(2,1)} %param.8), kind=kOutput, calls=%fused_computation.30 | convolution fusion | flops 2415919104 | bytes 9175040 | tf_op jit(solution)/shard_map/dot_general | solution.py:63
  18.3 4.7 %fusion.66 = bf16[512,1152]{1,0:T(8,128)(2,1)S(1)} fusion(f32[512,1152]{1,0:T(8,128)S(1)} %fusion.18, bf16[512,1792]{1,0:T(8,128)(2,1)S(1)} %copy-done.23, bf16[1792,4608]{1,0:T(8,128)(2,1)} %param.9, pred[]{:T(512)S(6)} %eq.24, bf16[512,2304]{1,0:T(8,128)(2,1)S(1)} %copy-done.20), kind=kOutput, calls=%fused_computation.62 | convolution fusion | flops 2116878336 | bytes 10682369 | tf_op jit(solution)/shard_map/dot_general | solution.py:63
  23.0 17.2 %collective-permute-done = bf16[512,1152]{1,0:T(8,128)(2,1)} collective-permute-done((bf16[512,1152]{1,0:T(8,128)(2,1)S(1)}, bf16[512,1152]{1,0:T(8,128)(2,1)}, u32[]{:S(2)}, u32[]{:S(2)}) %collective-permute-start) | collective-permute-done | bytes 1179680 | tf_op jit(solution)/shard_map/ppermute | solution.py:71
  40.2 1.5 add_convert_fusion.13
  41.8 2.3 fusion
  44.1 3.1 convolution_convert_fusion.3
  48.8 5.2 %fusion.20 = f32[512,1152]{1,0:T(8,128)S(1)} fusion(bf16[512,2048]{1,0:T(8,128)(2,1)S(1)} %copy-done, bf16[2048,4608]{1,0:T(8,128)(2,1)} %param.8), kind=kOutput, calls=%fused_computation.32 | convolution fusion | flops 2415919104 | bytes 9175040 | tf_op jit(solution)/shard_map/dot_general | solution.py:63
  54.0 4.7 %fusion.63 = bf16[512,1152]{1,0:T(8,128)(2,1)S(1)} fusion(f32[512,1152]{1,0:T(8,128)S(1)} %fusion.20, bf16[512,1792]{1,0:T(8,128)(2,1)S(1)} %copy-done.23, bf16[1792,4608]{1,0:T(8,128)(2,1)} %param.9, pred[]{:T(512)S(6)} %eq.23, bf16[512,2304]{1,0:T(8,128)(2,1)S(1)} %copy-done.20), kind=kOutput, calls=%fused_computation.61 | convolution fusion | flops 2116878336 | bytes 10682369 | tf_op jit(solution)/shard_map/dot_general | solution.py:63
  58.7 17.5 %collective-permute-done.1 = bf16[512,1152]{1,0:T(8,128)(2,1)S(1)} collective-permute-done((bf16[512,1152]{1,0:T(8,128)(2,1)S(1)}, bf16[512,1152]{1,0:T(8,128)(2,1)S(1)}, u32[]{:S(2)}, u32[]{:S(2)}) %collective-permute-start.1) | collective-permute-done | bytes 1179680 | tf_op jit(solution)/shard_map/ppermute | solution.py:71
  76.5 2.3 fusion.1
  79.1 3.3 convolution_convert_fusion.2
  82.4 1.9 dynamic-slice_bitcast_fusion.2
  86.3 5.5 %fusion.16 = f32[512,1152]{1,0:T(8,128)S(1)} fusion(bf16[512,2048]{1,0:T(8,128)(2,1)S(1)} %copy-done, bf16[2048,4608]{1,0:T(8,128)(2,1)} %param.8), kind=kOutput, calls=%fused_computation.28 | convolution fusion | flops 2415919104 | bytes 9175040 | tf_op jit(solution)/shard_map/dot_general | solution.py:63
  91.8 4.7 %fusion.69 = bf16[512,1152]{1,0:T(8,128)(2,1)S(1)} fusion(f32[512,1152]{1,0:T(8,128)S(1)} %fusion.16, bf16[512,1792]{1,0:T(8,128)(2,1)S(1)} %copy-done.24, bf16[1792,4608]{1,0:T(8,128)(2,1)} %param.9, pred[]{:T(512)S(6)} %eq.24, bf16[512,2304]{1,0:T(8,128)(2,1)S(1)} %copy-done.21), kind=kOutput, calls=%fused_computation.63 | convolution fusion | flops 2116878336 | bytes 10682369 | tf_op jit(solution)/shard_map/dot_general | solution.py:63
  97.1 1.6 collective-permute-start.14
  100.5 13.2 %collective-permute-done.2 = bf16[512,1152]{1,0:T(8,128)(2,1)S(1)} collective-permute-done((bf16[512,1152]{1,0:T(8,128)(2,1)S(1)}, bf16[512,1152]{1,0:T(8,128)(2,1)S(1)}, u32[]{:S(2)}, u32[]{:S(2)}) %collective-permute-start.2) | collective-permute-done | bytes 1179680 | tf_op jit(solution)/shard_map/ppermute | solution.py:71
  114.0 2.3 fusion.3
  116.4 1.6 dynamic-slice_bitcast_fusion.4
  118.9 2.9 convolution_convert_fusion
  121.8 2.0 dynamic-slice_bitcast_fusion
  128.4 24.8 %collective-permute-done.3 = bf16[512,1152]{1,0:T(8,128)(2,1)S(1)} collective-permute-done((bf16[512,1152]{1,0:T(8,128)(2,1)S(1)}, bf16[512,1152]{1,0:T(8,128)(2,1)S(1)}, u32[]{:S(2)}, u32[]{:S(2)}) %collective-permute-start.3) | collective-permute-done | bytes 1179680 | tf_op jit(solution)/shard_map/ppermute | solution.py:71
  153.2 1.5 collective-permute-start.15
  154.9 4.4 fusion.2
  159.3 4.3 convolution_convert_fusion.1
  163.6 1.5 collective-permute-start.29
  165.6 15.8 %fusion.72 = bf16[512,2048]{1,0:T(8,128)(2,1)} fusion(bf16[2048,4608]{1,0:T(8,128)(2,1)} %param.8, bf16[512,1152]{1,0:T(8,128)(2,1)} %copy-done.15, bf16[512,1152]{1,0:T(8,128)(2,1)} %copy-done.17, bf16[512,1152]{1,0:T(8,128)(2,1)} %copy-done.16, bf16[512,1152]{1,0:T(8,128)(2,1)S(1)} %copy-done.14), kind=kOutput, calls=%fused_computation.64 | convolution fusion | flops 9683599360 | bytes 25690112 | tf_op jit(solution)/shard_map/dot_general | solution.py:112
  181.4 1.6 collective-permute-start.10
  182.9 3.4 fusion.13
  186.6 2.0 copy-done.6
  189.8 1.9 add_convert_fusion.23
  191.9 1.5 fusion.81
  193.9 2.1 fusion.25
  196.0 2.4 collective-permute-start.16
  198.4 3.4 fusion.14
  201.8 9.9 %collective-permute-done.10 = bf16[288,2048]{1,0:T(8,128)(2,1)S(1)} collective-permute-done((bf16[288,2048]{1,0:T(8,128)(2,1)S(1)}, bf16[288,2048]{1,0:T(8,128)(2,1)S(1)}, u32[]{:S(2)}, u32[]{:S(2)}) %collective-permute-start.10) | collective-permute-done | bytes 1179680 | tf_op jit(solution)/shard_map/ppermute | solution.py:97
  213.0 3.4 collective-permute-done.9
  216.4 2.6 collective-permute-start.17
  219.6 1.9 collective-permute-done.16
  222.5 1.3 collective-permute-start.11
  225.3 20.6 %collective-permute-done.17 = bf16[288,2048]{1,0:T(8,128)(2,1)S(1)} collective-permute-done((bf16[288,2048]{1,0:T(8,128)(2,1)S(1)}, bf16[288,2048]{1,0:T(8,128)(2,1)S(1)}, u32[]{:S(2)}, u32[]{:S(2)}) %collective-permute-start.17) | collective-permute-done | bytes 1179680 | tf_op jit(solution)/shard_map/ppermute | solution.py:97
  249.5 1.3 collective-permute-start.30
  251.3 1.3 collective-permute-start.24
  254.3 19.2 %collective-permute-done.30 = bf16[288,1792]{1,0:T(8,128)(2,1)S(1)} collective-permute-done((bf16[288,1792]{1,0:T(8,128)(2,1)S(1)}, bf16[288,1792]{1,0:T(8,128)(2,1)S(1)}, u32[]{:S(2)}, u32[]{:S(2)}) %collective-permute-start.30) | collective-permute-done | bytes 1032224 | tf_op jit(solution)/shard_map/ppermute | solution.py:127
  273.7 23.3 %collective-permute-done.24 = bf16[288,2048]{1,0:T(8,128)(2,1)S(1)} collective-permute-done((bf16[288,2048]{1,0:T(8,128)(2,1)S(1)}, bf16[288,2048]{1,0:T(8,128)(2,1)S(1)}, u32[]{:S(2)}, u32[]{:S(2)}) %collective-permute-start.24) | collective-permute-done | bytes 1179680 | tf_op jit(solution)/shard_map/ppermute | solution.py:97
  297.6 1.3 collective-permute-start.33
  299.0 1.5 add_convert_fusion.6
  304.3 4.7 %collective-permute-start.39 = (bf16[288,1792]{1,0:T(8,128)(2,1)S(1)}, bf16[288,1792]{1,0:T(8,128)(2,1)S(1)}, u32[]{:S(2)}, u32[]{:S(2)}) collective-permute-start(bf16[288,1792]{1,0:T(8,128)(2,1)S(1)} %add_convert_fusion.15), channel_id=1, source_target_pairs={{16,24},{18,26},{20,28},{22,30},{17,25},{19,27},{21,29},{23,31}} | collective-permute-start | bytes 3096584 | tf_op jit(solution)/shard_map/ppermute | solution.py:97
  309.0 14.4 %collective-permute-done.33 = bf16[288,1792]{1,0:T(8,128)(2,1)S(1)} collective-permute-done((bf16[288,1792]{1,0:T(8,128)(2,1)S(1)}, bf16[288,1792]{1,0:T(8,128)(2,1)S(1)}, u32[]{:S(2)}, u32[]{:S(2)}) %collective-permute-start.33) | collective-permute-done | bytes 1032224 | tf_op jit(solution)/shard_map/ppermute | solution.py:127
  323.4 2.3 collective-permute-start.25
  326.0 20.1 %collective-permute-done.19 = bf16[288,2048]{1,0:T(8,128)(2,1)S(1)} collective-permute-done((bf16[288,2048]{1,0:T(8,128)(2,1)S(1)}, bf16[288,2048]{1,0:T(8,128)(2,1)S(1)}, u32[]{:S(2)}, u32[]{:S(2)}) %collective-permute-start.19) | collective-permute-done | bytes 1179680 | tf_op jit(solution)/shard_map/ppermute | solution.py:127
  347.8 6.3 %collective-permute-done.36 = bf16[288,1792]{1,0:T(8,128)(2,1)S(1)} collective-permute-done((bf16[288,1792]{1,0:T(8,128)(2,1)S(1)}, bf16[288,1792]{1,0:T(8,128)(2,1)S(1)}, u32[]{:S(2)}, u32[]{:S(2)}) %collective-permute-start.36) | collective-permute-done | bytes 1032224 | tf_op jit(solution)/shard_map/ppermute | solution.py:97
  356.6 19.6 %collective-permute-done.34 = bf16[288,1792]{1,0:T(8,128)(2,1)S(1)} collective-permute-done((bf16[288,1792]{1,0:T(8,128)(2,1)S(1)}, bf16[288,1792]{1,0:T(8,128)(2,1)S(1)}, u32[]{:S(2)}, u32[]{:S(2)}) %collective-permute-start.34) | collective-permute-done | bytes 1032224 | tf_op jit(solution)/shard_map/ppermute | solution.py:97
  376.2 2.4 collective-permute-start.37
  381.6 16.9 %collective-permute-done.20 = bf16[288,2048]{1,0:T(8,128)(2,1)S(1)} collective-permute-done((bf16[288,2048]{1,0:T(8,128)(2,1)S(1)}, bf16[288,2048]{1,0:T(8,128)(2,1)S(1)}, u32[]{:S(2)}, u32[]{:S(2)}) %collective-permute-start.20) | collective-permute-done | bytes 1179680 | tf_op jit(solution)/shard_map/ppermute | solution.py:97
  398.5 2.5 collective-permute-start.23
  401.0 1.5 add_convert_fusion.5
  403.4 1.5 collective-permute-start.21
  405.0 5.0 %fusion.88 = bf16[1792,288]{0,1:T(8,128)(2,1)} fusion(bf16[288,1792]{1,0:T(8,128)(2,1)} %collective-permute-done.35, bf16[288,1792]{1,0:T(8,128)(2,1)} %add_convert_fusion.19, bf16[288,1792]{1,0:T(8,128)(2,1)} %collective-permute-done.37, bf16[288,1792]{1,0:T(8,128)(2,1)} %add_convert_fusion.17, bf16[288,1792]{1,0:T(8,128)(2,1)} %add_convert_fusion.20, ...), kind=kLoop, calls=%fused_computation.126 | loop fusion | flops 7741440 | bytes 8257539 | tf_op jit(solution)/shard_map/transpose | solution.py:137
  410.1 12.6 %collective-permute-done.23 = bf16[288,2048]{1,0:T(8,128)(2,1)} collective-permute-done((bf16[288,2048]{1,0:T(8,128)(2,1)S(1)}, bf16[288,2048]{1,0:T(8,128)(2,1)}, u32[]{:S(2)}, u32[]{:S(2)}) %collective-permute-start.23) | collective-permute-done | bytes 1179680 | tf_op jit(solution)/shard_map/ppermute | solution.py:97
  422.6 7.9 %collective-permute-done.21 = bf16[288,2048]{1,0:T(8,128)(2,1)} collective-permute-done((bf16[288,2048]{1,0:T(8,128)(2,1)}, bf16[288,2048]{1,0:T(8,128)(2,1)}, u32[]{:S(2)}, u32[]{:S(2)}) %collective-permute-start.21) | collective-permute-done | bytes 1179680 | tf_op jit(solution)/shard_map/ppermute | solution.py:97
  430.5 5.5 %fusion.84 = bf16[2048,288]{0,1:T(8,128)(2,1)} fusion(bf16[288,2048]{1,0:T(8,128)(2,1)} %collective-permute-done.21, bf16[288,2048]{1,0:T(8,128)(2,1)} %add_convert_fusion.5, bf16[288,2048]{1,0:T(8,128)(2,1)} %collective-permute-done.23, bf16[288,2048]{1,0:T(8,128)(2,1)} %copy-done.5, bf16[288,2048]{1,0:T(8,128)(2,1)S(1)} %copy-done.4, ...), kind=kLoop, calls=%fused_computation.118 | loop fusion | flops 8847360 | bytes 9437187 | tf_op jit(solution)/shard_map/transpose | solution.py:137
  (135 shorter events, 38.6 us)
Async XLA Ops:
  0.6 1.6 copy-start
  2.2 5.4 %copy-start.19 = (bf16[512,2304]{1,0:T(8,128)(2,1)S(1)}, bf16[512,2304]{1,0:T(8,128)(2,1)}, u32[]{:S(2)}) copy-start(bf16[512,2304]{1,0:T(8,128)(2,1)} %param.5) | copy-start | bytes 7077892
  2.2 5.4 %copy-start.22 = (bf16[512,1792]{1,0:T(8,128)(2,1)S(1)}, bf16[512,1792]{1,0:T(8,128)(2,1)}, u32[]{:S(2)}) copy-start(bf16[512,1792]{1,0:T(8,128)(2,1)} %param.7) | copy-start | bytes 5505028
  12.3 27.9 %collective-permute-start = (bf16[512,1152]{1,0:T(8,128)(2,1)S(1)}, bf16[512,1152]{1,0:T(8,128)(2,1)}, u32[]{:S(2)}, u32[]{:S(2)}) collective-permute-start(bf16[512,1152]{1,0:T(8,128)(2,1)S(1)} %fusion.60), channel_id=1, source_target_pairs={{0,1},{1,0},{2,3},{3,2},{4,5},{5,4},{6,7},{7,6},{8,9},{9,8},{10,11... | collective-permute-start | bytes 3538952 | tf_op jit(solution)/shard_map/ppermute | solution.py:71
  12.9 5.4 %copy-start.20 = (bf16[512,2304]{1,0:T(8,128)(2,1)S(1)}, bf16[512,2304]{1,0:T(8,128)(2,1)}, u32[]{:S(2)}) copy-start(bf16[512,2304]{1,0:T(8,128)(2,1)} %param.5) | copy-start | bytes 7077892
  12.9 5.4 %copy-start.23 = (bf16[512,1792]{1,0:T(8,128)(2,1)S(1)}, bf16[512,1792]{1,0:T(8,128)(2,1)}, u32[]{:S(2)}) copy-start(bf16[512,1792]{1,0:T(8,128)(2,1)} %param.7) | copy-start | bytes 5505028
  41.8 2.4 copy-start.13
  47.4 49.2 %collective-permute-start.13 = (bf16[2,288,1792]{2,1,0:T(8,128)(2,1)S(1)}, bf16[2,288,1792]{2,1,0:T(8,128)(2,1)S(1)}, u32[]{:S(2)}, u32[]{:S(2)}) collective-permute-start(bf16[2,288,1792]{2,1,0:T(8,128)(2,1)S(1)} %dynamic-slice_bitcast_fusion.7), channel_id=1, source_target_pairs={{0,2},{2,0},{4,6},{6,4},{8,10},{10,8},{12,14},{14,12},{16,18},{18,... | collective-permute-start | bytes 6193160 | tf_op jit(solution)/shard_map/ppermute | solution.py:109
  47.7 50.9 %collective-permute-start.7 = (bf16[2,288,2048]{2,1,0:T(8,128)(2,1)S(1)}, bf16[2,288,2048]{2,1,0:T(8,128)(2,1)S(1)}, u32[]{:S(2)}, u32[]{:S(2)}) collective-permute-start(bf16[2,288,2048]{2,1,0:T(8,128)(2,1)S(1)} %dynamic-slice_bitcast_fusion.3), channel_id=1, source_target_pairs={{0,2},{2,0},{4,6},{6,4},{8,10},{10,8},{12,14},{14,12},{16,18},{18,... | collective-permute-start | bytes 7077896 | tf_op jit(solution)/shard_map/ppermute | solution.py:109
  48.3 28.0 %collective-permute-start.1 = (bf16[512,1152]{1,0:T(8,128)(2,1)S(1)}, bf16[512,1152]{1,0:T(8,128)(2,1)S(1)}, u32[]{:S(2)}, u32[]{:S(2)}) collective-permute-start(bf16[512,1152]{1,0:T(8,128)(2,1)S(1)} %fusion.66), channel_id=1, source_target_pairs={{0,1},{1,0},{2,3},{3,2},{4,5},{5,4},{6,7},{7,6},{8,9},{9,8},{10,11... | collective-permute-start | bytes 3538952 | tf_op jit(solution)/shard_map/ppermute | solution.py:71
  76.5 2.6 copy-start.15
  79.0 47.5 %collective-permute-start.28 = (bf16[2,288,1792]{2,1,0:T(8,128)(2,1)S(1)}, bf16[2,288,1792]{2,1,0:T(8,128)(2,1)S(1)}, u32[]{:S(2)}, u32[]{:S(2)}) collective-permute-start(bf16[2,288,1792]{2,1,0:T(8,128)(2,1)S(1)} %dynamic-slice_bitcast_fusion.6), channel_id=1, source_target_pairs={{0,2},{2,0},{4,6},{6,4},{8,10},{10,8},{12,14},{14,12},{16,18},{18,... | collective-permute-start | bytes 6193160 | tf_op jit(solution)/shard_map/ppermute | solution.py:109
  82.4 2.9 copy-start.7
  85.3 6.5 %copy-start.24 = (bf16[512,1792]{1,0:T(8,128)(2,1)S(1)}, bf16[512,1792]{1,0:T(8,128)(2,1)}, u32[]{:S(2)}) copy-start(bf16[512,1792]{1,0:T(8,128)(2,1)} %param.7) | copy-start | bytes 5505028
  85.3 96.0 %collective-permute-start.6 = (bf16[2,288,2048]{2,1,0:T(8,128)(2,1)}, bf16[2,288,2048]{2,1,0:T(8,128)(2,1)}, u32[]{:S(2)}, u32[]{:S(2)}) collective-permute-start(bf16[2,288,2048]{2,1,0:T(8,128)(2,1)} %dynamic-slice_bitcast_fusion.2), channel_id=1, source_target_pairs={{0,2},{2,0},{4,6},{6,4},{8,10},{10,8},{12,14},{14,12},{16,18},{18,... | collective-permute-start | bytes 7077896 | tf_op jit(solution)/shard_map/ppermute | solution.py:109
  85.8 6.0 %copy-start.21 = (bf16[512,2304]{1,0:T(8,128)(2,1)S(1)}, bf16[512,2304]{1,0:T(8,128)(2,1)}, u32[]{:S(2)}) copy-start(bf16[512,2304]{1,0:T(8,128)(2,1)} %param.5) | copy-start | bytes 7077892
  85.8 27.9 %collective-permute-start.2 = (bf16[512,1152]{1,0:T(8,128)(2,1)S(1)}, bf16[512,1152]{1,0:T(8,128)(2,1)S(1)}, u32[]{:S(2)}, u32[]{:S(2)}) collective-permute-start(bf16[512,1152]{1,0:T(8,128)(2,1)S(1)} %fusion.63), channel_id=1, source_target_pairs={{0,1},{1,0},{2,3},{3,2},{4,5},{5,4},{6,7},{7,6},{8,9},{9,8},{10,11... | collective-permute-start | bytes 3538952 | tf_op jit(solution)/shard_map/ppermute | solution.py:71
  97.1 27.7 %collective-permute-start.14 = (bf16[288,1792]{1,0:T(8,128)(2,1)S(1)}, bf16[288,1792]{1,0:T(8,128)(2,1)S(1)}, u32[]{:S(2)}, u32[]{:S(2)}) collective-permute-start(bf16[288,1792]{1,0:T(8,128)(2,1)S(1)} %dynamic-slice_bitcast_fusion.15), channel_id=1, source_target_pairs={{0,4},{2,6},{4,0},{6,2},{8,12},{10,14},{12,8},{14,10},{16,20},{18,... | collective-permute-start | bytes 3096584 | tf_op jit(solution)/shard_map/ppermute | solution.py:127
  99.9 63.8 %collective-permute-start.8 = (bf16[288,2048]{1,0:T(8,128)(2,1)S(1)}, bf16[288,2048]{1,0:T(8,128)(2,1)S(1)}, u32[]{:S(2)}, u32[]{:S(2)}) collective-permute-start(bf16[288,2048]{1,0:T(8,128)(2,1)S(1)} %dynamic-slice_bitcast_fusion.11), channel_id=1, source_target_pairs={{0,4},{2,6},{4,0},{6,2},{8,12},{10,14},{12,8},{14,10},{16,20},{18,... | collective-permute-start | bytes 3538952 | tf_op jit(solution)/shard_map/ppermute | solution.py:127
  114.0 4.9 %copy-start.16 = (bf16[512,1152]{1,0:T(8,128)(2,1)}, bf16[512,1152]{1,0:T(8,128)(2,1)S(1)}, u32[]{:S(2)}) copy-start(bf16[512,1152]{1,0:T(8,128)(2,1)S(1)} %add_convert_fusion.11) | copy-start | bytes 3538948
  116.3 2.6 copy-start.11
  118.9 74.4 %collective-permute-start.27 = (bf16[2,288,1792]{2,1,0:T(8,128)(2,1)}, bf16[2,288,1792]{2,1,0:T(8,128)(2,1)}, u32[]{:S(2)}, u32[]{:S(2)}) collective-permute-start(bf16[2,288,1792]{2,1,0:T(8,128)(2,1)} %dynamic-slice_bitcast_fusion.4), channel_id=1, source_target_pairs={{0,2},{2,0},{4,6},{6,4},{8,10},{10,8},{12,14},{14,12},{16,18},{18,... | collective-permute-start | bytes 6193160 | tf_op jit(solution)/shard_map/ppermute | solution.py:109
  121.8 3.0 copy-start.8
  124.8 28.4 %collective-permute-start.3 = (bf16[512,1152]{1,0:T(8,128)(2,1)S(1)}, bf16[512,1152]{1,0:T(8,128)(2,1)S(1)}, u32[]{:S(2)}, u32[]{:S(2)}) collective-permute-start(bf16[512,1152]{1,0:T(8,128)(2,1)S(1)} %fusion.69), channel_id=1, source_target_pairs={{0,1},{1,0},{2,3},{3,2},{4,5},{5,4},{6,7},{7,6},{8,9},{9,8},{10,11... | collective-permute-start | bytes 3538952 | tf_op jit(solution)/shard_map/ppermute | solution.py:71
  126.5 69.4 %collective-permute-start.5 = (bf16[2,288,2048]{2,1,0:T(8,128)(2,1)}, bf16[2,288,2048]{2,1,0:T(8,128)(2,1)}, u32[]{:S(2)}, u32[]{:S(2)}) collective-permute-start(bf16[2,288,2048]{2,1,0:T(8,128)(2,1)} %dynamic-slice_bitcast_fusion), channel_id=1, source_target_pairs={{0,2},{2,0},{4,6},{6,4},{8,10},{10,8},{12,14},{14,12},{16,18},{18,... | collective-permute-start | bytes 7077896 | tf_op jit(solution)/shard_map/ppermute | solution.py:109
  127.2 27.7 %copy-start.2 = (bf16[2,288,1792]{2,1,0:T(8,128)(2,1)}, bf16[2,288,1792]{2,1,0:T(8,128)(2,1)S(1)}, u32[]{:S(2)}) copy-start(bf16[2,288,1792]{2,1,0:T(8,128)(2,1)S(1)} %fusion.24) | copy-start | bytes 6193156
  153.2 35.8 %collective-permute-start.15 = (bf16[288,1792]{1,0:T(8,128)(2,1)}, bf16[288,1792]{1,0:T(8,128)(2,1)}, u32[]{:S(2)}, u32[]{:S(2)}) collective-permute-start(bf16[288,1792]{1,0:T(8,128)(2,1)} %fusion.82), channel_id=1, source_target_pairs={{24,16},{26,18},{28,20},{30,22},{25,17},{27,19},{29,21},{31,23}} | collective-permute-start | bytes 3096584 | tf_op jit(solution)/shard_map/ppermute | solution.py:97
  154.9 4.4 %copy-start.17 = (bf16[512,1152]{1,0:T(8,128)(2,1)}, bf16[512,1152]{1,0:T(8,128)(2,1)S(1)}, u32[]{:S(2)}) copy-start(bf16[512,1152]{1,0:T(8,128)(2,1)S(1)} %add_convert_fusion.10) | copy-start | bytes 3538948
  163.6 2.0 copy-start.14
  163.6 28.1 %collective-permute-start.29 = (bf16[288,1792]{1,0:T(8,128)(2,1)}, bf16[288,1792]{1,0:T(8,128)(2,1)}, u32[]{:S(2)}, u32[]{:S(2)}) collective-permute-start(bf16[288,1792]{1,0:T(8,128)(2,1)} %dynamic-slice_bitcast_fusion.14), channel_id=1, source_target_pairs={{0,4},{2,6},{4,0},{6,2},{8,12},{10,14},{12,8},{14,10},{16,20},{18,... | collective-permute-start | bytes 3096584 | tf_op jit(solution)/shard_map/ppermute | solution.py:127
  181.3 5.0 %copy-start.10 = (bf16[1152,1792]{1,0:T(8,128)(2,1)S(1)}, bf16[1152,1792]{1,0:T(8,128)(2,1)}, u32[]{:S(2)}) copy-start(bf16[1152,1792]{1,0:T(8,128)(2,1)} %fusion.2) | copy-start | bytes 12386308
  181.4 30.4 %collective-permute-start.10 = (bf16[288,2048]{1,0:T(8,128)(2,1)S(1)}, bf16[288,2048]{1,0:T(8,128)(2,1)S(1)}, u32[]{:S(2)}, u32[]{:S(2)}) collective-permute-start(bf16[288,2048]{1,0:T(8,128)(2,1)S(1)} %fusion.78), channel_id=1, source_target_pairs={{24,16},{26,18},{28,20},{30,22},{25,17},{27,19},{29,21},{31,23}} | collective-permute-start | bytes 3538952 | tf_op jit(solution)/shard_map/ppermute | solution.py:97
  186.4 2.3 copy-start.6
  189.0 2.9 copy-start.3
  189.0 27.4 %collective-permute-start.9 = (bf16[288,2048]{1,0:T(8,128)(2,1)S(1)}, bf16[288,2048]{1,0:T(8,128)(2,1)S(1)}, u32[]{:S(2)}, u32[]{:S(2)}) collective-permute-start(bf16[288,2048]{1,0:T(8,128)(2,1)S(1)} %dynamic-slice_bitcast_fusion.10), channel_id=1, source_target_pairs={{0,4},{2,6},{4,0},{6,2},{8,12},{10,14},{12,8},{14,10},{16,20},{18,... | collective-permute-start | bytes 3538952 | tf_op jit(solution)/shard_map/ppermute | solution.py:127
  189.8 4.1 copy-start.12
  191.8 32.3 %collective-permute-start.26 = (bf16[2,288,1792]{2,1,0:T(8,128)(2,1)S(1)}, bf16[2,288,1792]{2,1,0:T(8,128)(2,1)S(1)}, u32[]{:S(2)}, u32[]{:S(2)}) collective-permute-start(bf16[2,288,1792]{2,1,0:T(8,128)(2,1)S(1)} %dynamic-slice_bitcast_fusion.5), channel_id=1, source_target_pairs={{0,2},{2,0},{4,6},{6,4},{8,10},{10,8},{12,14},{14,12},{16,18},{18,... | collective-permute-start | bytes 6193160 | tf_op jit(solution)/shard_map/ppermute | solution.py:109
  193.3 54.3 %collective-permute-start.4 = (bf16[2,288,2048]{2,1,0:T(8,128)(2,1)S(1)}, bf16[2,288,2048]{2,1,0:T(8,128)(2,1)S(1)}, u32[]{:S(2)}, u32[]{:S(2)}) collective-permute-start(bf16[2,288,2048]{2,1,0:T(8,128)(2,1)S(1)} %dynamic-slice_bitcast_fusion.1), channel_id=1, source_target_pairs={{0,2},{2,0},{4,6},{6,4},{8,10},{10,8},{12,14},{14,12},{16,18},{18,... | collective-permute-start | bytes 7077896 | tf_op jit(solution)/shard_map/ppermute | solution.py:109
  196.0 25.5 %collective-permute-start.16 = (bf16[288,1792]{1,0:T(8,128)(2,1)S(1)}, bf16[288,1792]{1,0:T(8,128)(2,1)S(1)}, u32[]{:S(2)}, u32[]{:S(2)}) collective-permute-start(bf16[288,1792]{1,0:T(8,128)(2,1)S(1)} %add_convert_fusion.23), channel_id=1, source_target_pairs={{16,8},{18,10},{20,12},{22,14},{17,9},{19,11},{21,13},{23,15}} | collective-permute-start | bytes 3096584 | tf_op jit(solution)/shard_map/ppermute | solution.py:97
  211.8 10.7 %collective-permute-start.31 = (bf16[288,1792]{1,0:T(8,128)(2,1)S(1)}, bf16[288,1792]{1,0:T(8,128)(2,1)S(1)}, u32[]{:S(2)}, u32[]{:S(2)}) collective-permute-start(bf16[288,1792]{1,0:T(8,128)(2,1)S(1)} %fusion.81), channel_id=1, source_target_pairs={{0,8},{2,10},{4,12},{6,14},{1,9},{3,11},{5,13},{7,15}} | collective-permute-start | bytes 3096584 | tf_op jit(solution)/shard_map/ppermute | solution.py:97
  216.4 29.5 %collective-permute-start.17 = (bf16[288,2048]{1,0:T(8,128)(2,1)S(1)}, bf16[288,2048]{1,0:T(8,128)(2,1)S(1)}, u32[]{:S(2)}, u32[]{:S(2)}) collective-permute-start(bf16[288,2048]{1,0:T(8,128)(2,1)S(1)} %add_convert_fusion.9), channel_id=1, source_target_pairs={{16,8},{18,10},{20,12},{22,14},{17,9},{19,11},{21,13},{23,15}} | collective-permute-start | bytes 3538952 | tf_op jit(solution)/shard_map/ppermute | solution.py:97
  221.5 28.0 %collective-permute-start.12 = (bf16[288,2048]{1,0:T(8,128)(2,1)S(1)}, bf16[288,2048]{1,0:T(8,128)(2,1)S(1)}, u32[]{:S(2)}, u32[]{:S(2)}) collective-permute-start(bf16[288,2048]{1,0:T(8,128)(2,1)S(1)} %fusion.77), channel_id=1, source_target_pairs={{0,8},{2,10},{4,12},{6,14},{1,9},{3,11},{5,13},{7,15}} | collective-permute-start | bytes 3538952 | tf_op jit(solution)/shard_map/ppermute | solution.py:97
  222.5 28.8 %collective-permute-start.11 = (bf16[288,2048]{1,0:T(8,128)(2,1)S(1)}, bf16[288,2048]{1,0:T(8,128)(2,1)S(1)}, u32[]{:S(2)}, u32[]{:S(2)}) collective-permute-start(bf16[288,2048]{1,0:T(8,128)(2,1)S(1)} %dynamic-slice_bitcast_fusion.9), channel_id=1, source_target_pairs={{0,4},{2,6},{4,0},{6,2},{8,12},{10,14},{12,8},{14,10},{16,20},{18,... | collective-permute-start | bytes 3538952 | tf_op jit(solution)/shard_map/ppermute | solution.py:127
  224.0 29.0 %collective-permute-start.32 = (bf16[288,1792]{1,0:T(8,128)(2,1)S(1)}, bf16[288,1792]{1,0:T(8,128)(2,1)S(1)}, u32[]{:S(2)}, u32[]{:S(2)}) collective-permute-start(bf16[288,1792]{1,0:T(8,128)(2,1)S(1)} %add_convert_fusion.22), channel_id=1, source_target_pairs={{8,0},{10,2},{12,4},{14,6},{9,1},{11,3},{13,5},{15,7}} | collective-permute-start | bytes 3096584 | tf_op jit(solution)/shard_map/ppermute | solution.py:97
  245.8 58.1 %collective-permute-start.38 = (bf16[288,1792]{1,0:T(8,128)(2,1)S(1)}, bf16[288,1792]{1,0:T(8,128)(2,1)S(1)}, u32[]{:S(2)}, u32[]{:S(2)}) collective-permute-start(bf16[288,1792]{1,0:T(8,128)(2,1)S(1)} %add_convert_fusion.21), channel_id=1, source_target_pairs={{8,16},{10,18},{12,20},{14,22},{9,17},{11,19},{13,21},{15,23}} | collective-permute-start | bytes 3096584 | tf_op jit(solution)/shard_map/ppermute | solution.py:97
  247.7 51.3 %collective-permute-start.18 = (bf16[288,2048]{1,0:T(8,128)(2,1)S(1)}, bf16[288,2048]{1,0:T(8,128)(2,1)S(1)}, u32[]{:S(2)}, u32[]{:S(2)}) collective-permute-start(bf16[288,2048]{1,0:T(8,128)(2,1)S(1)} %add_convert_fusion.7), channel_id=1, source_target_pairs={{8,0},{10,2},{12,4},{14,6},{9,1},{11,3},{13,5},{15,7}} | collective-permute-start | bytes 3538952 | tf_op jit(solution)/shard_map/ppermute | solution.py:97
  249.5 24.0 %collective-permute-start.30 = (bf16[288,1792]{1,0:T(8,128)(2,1)S(1)}, bf16[288,1792]{1,0:T(8,128)(2,1)S(1)}, u32[]{:S(2)}, u32[]{:S(2)}) collective-permute-start(bf16[288,1792]{1,0:T(8,128)(2,1)S(1)} %dynamic-slice_bitcast_fusion.13), channel_id=1, source_target_pairs={{0,4},{2,6},{4,0},{6,2},{8,12},{10,14},{12,8},{14,10},{16,20},{18,... | collective-permute-start | bytes 3096584 | tf_op jit(solution)/shard_map/ppermute | solution.py:127
  251.3 45.7 %collective-permute-start.24 = (bf16[288,2048]{1,0:T(8,128)(2,1)S(1)}, bf16[288,2048]{1,0:T(8,128)(2,1)S(1)}, u32[]{:S(2)}, u32[]{:S(2)}) collective-permute-start(bf16[288,2048]{1,0:T(8,128)(2,1)S(1)} %add_convert_fusion.8), channel_id=1, source_target_pairs={{8,16},{10,18},{12,20},{14,22},{9,17},{11,19},{13,21},{15,23}} | collective-permute-start | bytes 3538952 | tf_op jit(solution)/shard_map/ppermute | solution.py:97
  297.6 25.8 %collective-permute-start.33 = (bf16[288,1792]{1,0:T(8,128)(2,1)S(1)}, bf16[288,1792]{1,0:T(8,128)(2,1)S(1)}, u32[]{:S(2)}, u32[]{:S(2)}) collective-permute-start(bf16[288,1792]{1,0:T(8,128)(2,1)S(1)} %dynamic-slice_bitcast_fusion.12), channel_id=1, source_target_pairs={{0,4},{2,6},{4,0},{6,2},{8,12},{10,14},{12,8},{14,10},{16,20},{18,... | collective-permute-start | bytes 3096584 | tf_op jit(solution)/shard_map/ppermute | solution.py:127
  300.6 45.5 %collective-permute-start.19 = (bf16[288,2048]{1,0:T(8,128)(2,1)S(1)}, bf16[288,2048]{1,0:T(8,128)(2,1)S(1)}, u32[]{:S(2)}, u32[]{:S(2)}) collective-permute-start(bf16[288,2048]{1,0:T(8,128)(2,1)S(1)} %dynamic-slice_bitcast_fusion.8), channel_id=1, source_target_pairs={{0,4},{2,6},{4,0},{6,2},{8,12},{10,14},{12,8},{14,10},{16,20},{18,... | collective-permute-start | bytes 3538952 | tf_op jit(solution)/shard_map/ppermute | solution.py:127
  301.4 78.5 %collective-permute-start.22 = (bf16[288,2048]{1,0:T(8,128)(2,1)S(1)}, bf16[288,2048]{1,0:T(8,128)(2,1)S(1)}, u32[]{:S(2)}, u32[]{:S(2)}) collective-permute-start(bf16[288,2048]{1,0:T(8,128)(2,1)S(1)} %fusion.76), channel_id=1, source_target_pairs={{24,16},{26,18},{28,20},{30,22},{0,8},{2,10},{4,12},{6,14},{25,17}... | collective-permute-start | bytes 3538952 | tf_op jit(solution)/shard_map/ppermute | solution.py:97
  302.7 51.4 %collective-permute-start.36 = (bf16[288,1792]{1,0:T(8,128)(2,1)S(1)}, bf16[288,1792]{1,0:T(8,128)(2,1)S(1)}, u32[]{:S(2)}, u32[]{:S(2)}) collective-permute-start(bf16[288,1792]{1,0:T(8,128)(2,1)S(1)} %fusion.80), channel_id=1, source_target_pairs={{24,16},{26,18},{28,20},{30,22},{0,8},{2,10},{4,12},{6,14},{25,17}... | collective-permute-start | bytes 3096584 | tf_op jit(solution)/shard_map/ppermute | solution.py:97
  304.2 43.6 %copy-start.9 = (bf16[288,1792]{1,0:T(8,128)(2,1)}, bf16[288,1792]{1,0:T(8,128)(2,1)S(1)}, u32[]{:S(2)}) copy-start(bf16[288,1792]{1,0:T(8,128)(2,1)S(1)} %add_convert_fusion.15) | copy-start | bytes 3096580
  304.3 98.2 %collective-permute-start.39 = (bf16[288,1792]{1,0:T(8,128)(2,1)S(1)}, bf16[288,1792]{1,0:T(8,128)(2,1)S(1)}, u32[]{:S(2)}, u32[]{:S(2)}) collective-permute-start(bf16[288,1792]{1,0:T(8,128)(2,1)S(1)} %add_convert_fusion.15), channel_id=1, source_target_pairs={{16,24},{18,26},{20,28},{22,30},{17,25},{19,27},{21,29},{23,31}} | collective-permute-start | bytes 3096584 | tf_op jit(solution)/shard_map/ppermute | solution.py:97
  323.4 86.6 %collective-permute-start.25 = (bf16[288,2048]{1,0:T(8,128)(2,1)S(1)}, bf16[288,2048]{1,0:T(8,128)(2,1)}, u32[]{:S(2)}, u32[]{:S(2)}) collective-permute-start(bf16[288,2048]{1,0:T(8,128)(2,1)S(1)} %add_convert_fusion.1), channel_id=1, source_target_pairs={{16,24},{18,26},{20,28},{22,30},{17,25},{19,27},{21,29},{23,31}} | collective-permute-start | bytes 3538952 | tf_op jit(solution)/shard_map/ppermute | solution.py:97
  346.1 30.2 %collective-permute-start.34 = (bf16[288,1792]{1,0:T(8,128)(2,1)S(1)}, bf16[288,1792]{1,0:T(8,128)(2,1)S(1)}, u32[]{:S(2)}, u32[]{:S(2)}) collective-permute-start(bf16[288,1792]{1,0:T(8,128)(2,1)S(1)} %fusion.79), channel_id=1, source_target_pairs={{0,8},{2,10},{4,12},{6,14},{24,16},{26,18},{28,20},{30,22},{1,9},{... | collective-permute-start | bytes 3096584 | tf_op jit(solution)/shard_map/ppermute | solution.py:97
  354.1 44.4 %collective-permute-start.20 = (bf16[288,2048]{1,0:T(8,128)(2,1)S(1)}, bf16[288,2048]{1,0:T(8,128)(2,1)S(1)}, u32[]{:S(2)}, u32[]{:S(2)}) collective-permute-start(bf16[288,2048]{1,0:T(8,128)(2,1)S(1)} %fusion.75), channel_id=1, source_target_pairs={{0,8},{2,10},{4,12},{6,14},{24,16},{26,18},{28,20},{30,22},{1,9},{... | collective-permute-start | bytes 3538952 | tf_op jit(solution)/shard_map/ppermute | solution.py:97
  376.2 28.8 %collective-permute-start.37 = (bf16[288,1792]{1,0:T(8,128)(2,1)}, bf16[288,1792]{1,0:T(8,128)(2,1)}, u32[]{:S(2)}, u32[]{:S(2)}) collective-permute-start(bf16[288,1792]{1,0:T(8,128)(2,1)} %add_convert_fusion.17), channel_id=1, source_target_pairs={{16,8},{18,10},{20,12},{22,14},{17,9},{19,11},{21,13},{23,15}} | collective-permute-start | bytes 3096584 | tf_op jit(solution)/shard_map/ppermute | solution.py:97
  379.9 25.1 %collective-permute-start.35 = (bf16[288,1792]{1,0:T(8,128)(2,1)}, bf16[288,1792]{1,0:T(8,128)(2,1)}, u32[]{:S(2)}, u32[]{:S(2)}) collective-permute-start(bf16[288,1792]{1,0:T(8,128)(2,1)} %add_convert_fusion.19), channel_id=1, source_target_pairs={{8,16},{10,18},{12,20},{14,22},{9,17},{11,19},{13,21},{15,23}} | collective-permute-start | bytes 3096584 | tf_op jit(solution)/shard_map/ppermute | solution.py:97
  381.6 28.4 %copy-start.5 = (bf16[288,2048]{1,0:T(8,128)(2,1)}, bf16[288,2048]{1,0:T(8,128)(2,1)S(1)}, u32[]{:S(2)}) copy-start(bf16[288,2048]{1,0:T(8,128)(2,1)S(1)} %add_convert_fusion.3) | copy-start | bytes 3538948
  398.5 24.1 %collective-permute-start.23 = (bf16[288,2048]{1,0:T(8,128)(2,1)S(1)}, bf16[288,2048]{1,0:T(8,128)(2,1)}, u32[]{:S(2)}, u32[]{:S(2)}) collective-permute-start(bf16[288,2048]{1,0:T(8,128)(2,1)S(1)} %add_convert_fusion.3), channel_id=1, source_target_pairs={{16,8},{18,10},{20,12},{22,14},{17,9},{19,11},{21,13},{23,15}} | collective-permute-start | bytes 3538952 | tf_op jit(solution)/shard_map/ppermute | solution.py:97
  403.4 27.1 %collective-permute-start.21 = (bf16[288,2048]{1,0:T(8,128)(2,1)}, bf16[288,2048]{1,0:T(8,128)(2,1)}, u32[]{:S(2)}, u32[]{:S(2)}) collective-permute-start(bf16[288,2048]{1,0:T(8,128)(2,1)} %add_convert_fusion.5), channel_id=1, source_target_pairs={{8,16},{10,18},{12,20},{14,22},{9,17},{11,19},{13,21},{15,23}} | collective-permute-start | bytes 3538952 | tf_op jit(solution)/shard_map/ppermute | solution.py:97
  405.0 25.5 %copy-start.4 = (bf16[288,2048]{1,0:T(8,128)(2,1)S(1)}, bf16[288,2048]{1,0:T(8,128)(2,1)}, u32[]{:S(2)}) copy-start(bf16[288,2048]{1,0:T(8,128)(2,1)} %add_convert_fusion.6) | copy-start | bytes 3538948
  430.5 5.5 %copy-start.1 = (bf16[512,2048]{1,0:T(8,128)(2,1)S(1)}, bf16[512,2048]{1,0:T(8,128)(2,1)}, u32[]{:S(2)}) copy-start(bf16[512,2048]{1,0:T(8,128)(2,1)} %param.6) | copy-start | bytes 6291460
  (1 other events, 1.0 us)
